TPU v7x, 128 devices: a whole 4x4x4 slice. The times are simulated.
128 devices in a mesh: grp: 8 (over x, core), dev: 16 (over y, z).
Axes of the slice: x: 4, y: 4, z: 4, core: 2. Of those that a mesh axis runs over, the one named last changes fastest.
Arguments:
- node_features: float32 [65536, 768], P(('grp', 'dev')), may hold values from -6 to 6
- tiles: bfloat16 [6656, 128, 128], P(('grp', 'dev')), may hold values from -0.15625 to 0.15625
- tile_list: int32 [6656, 2], replicated, may hold values from 0 to 511, as said below
- weight: float32 [768, 768], replicated, may hold values from -0.21875 to 0.21875
- texts: float32 [4096, 768], P(('grp', 'dev')), may hold values from -6 to 6
- selected: int32 [4096], P(('grp', 'dev')), may hold values from 0 to 65535, as said below
- pairing: int32 [4096], P(('grp', 'dev')), may hold values from 0 to 4095, each once
Outputs:
- contrast_loss: float32 [], replicated
- grad_nodes: float32 [65536, 768], P(('grp', 'dev'))
- grad_weight: float32 [768, 768], replicated
- grad_texts: float32 [4096, 768], P(('grp', 'dev'))
Inputs may be any that keep to these rules, and one draw needn't show every extreme that they name: `tile_list`: device number p = grp index * (devices along dev) + dev index holds node blocks p * 4 to (p + 1) * 4 - 1 and tiles p * 52 to (p + 1) * 52 - 1. A tile's row block lies on the device that holds the tile; its column block lies on that device, on another device of the same grp index, or on the device of the same dev index in another grp. At most 2 tiles of one device have column blocks on any one other device; in every draw each device has one other device of its grp index and one of its dev index at that most. `selected`: distinct ids; the ids listed on a device are nodes of that device.
All inputs are finite; a program needn't handle non-finite values.
Results may differ from a plain program's by a relative error of at most 0.0004.
The roundings to bfloat16 on the way count: a program that leaves them out, or rounds other values in their place, can miss the bound.
Values may be sent and summed in bfloat16 or wider, within the bound.
A program may use at most 128 MiB of HBM per device.

v0:
```python
import functools

import jax
import jax.numpy as jnp
from jax import lax
from jax.sharding import Mesh
from jax.sharding import PartitionSpec as P

CAP = 2
GRP = ("grp_0", "grp_1")
DEV = ("dev_0", "dev_1")
GRP_DEV = ("grp_0", "grp_1", "dev_0", "dev_1")


SCALE = 1.0 / 0.07
EPS = 1e-06
PRECISE = lax.Precision.HIGHEST
ROOT_HALF = 0.7071067811865476
INV_ROOT_TWO_PI = 0.3989422804014327


def laid_out(blocks, dim):
    lengths = list(blocks.shape[1:])
    lengths[dim] *= blocks.shape[0]
    return jnp.moveaxis(blocks, 0, dim).reshape(lengths)


def from_everyone(array, axis):
    copies = jnp.broadcast_to(array, (lax.axis_size(axis), *array.shape))
    return lax.all_to_all(copies, axis, split_axis=0, concat_axis=0, tiled=True)


def gather_directly(array, axis, dim):
    return laid_out(from_everyone(array, axis), dim)


def over_axes(array, axes):
    return functools.reduce(lax.psum, axes, array)


def over_copies(array, axis):
    return from_everyone(array, axis).sum(axis=0)


def split_up(array, dim, length):
    lengths = array.shape
    blocks = array.reshape(*lengths[:dim], length, lengths[dim] // length, *lengths[dim + 1 :])
    return jnp.moveaxis(blocks, dim, 0)


def summed_on_arrival(array, axis, dim):
    length = lax.axis_size(axis)
    blocks = lax.all_to_all(split_up(array, dim, length), axis, 0, 0, tiled=True)
    return jnp.sum(blocks, axis=0)


def gelu_value(value):
    return 0.5 * value * (1.0 + lax.erf(value * ROOT_HALF))


def gelu_slope(value):
    return (
        0.5 * (1.0 + lax.erf(value * ROOT_HALF))
        + value * jnp.exp(-0.5 * value * value) * INV_ROOT_TWO_PI
    )


def slot_plan(peer_lists, peer_ids, device, blocks_dev, capacity):
    col_owner = peer_lists[:, :, 1] // blocks_dev
    wanted = (col_owner == device) & (peer_ids[:, None] != device)
    slot_order = jnp.cumsum(wanted.astype(jnp.int32), axis=1) - 1
    local_block = peer_lists[:, :, 1] - device * blocks_dev
    slot_hits = wanted[:, :, None] & (
        slot_order[:, :, None] == jnp.arange(capacity, dtype=jnp.int32)[None, None, :]
    )
    block_index = jnp.sum(jnp.where(slot_hits, local_block[:, :, None], 0), axis=1)
    slot_valid = jnp.any(slot_hits, axis=1)
    return (block_index.reshape(-1), slot_valid.reshape(-1))


def slot_pick(slot_of_tile, keep, slots_all):
    return (slot_of_tile[None, :] == jnp.arange(slots_all, dtype=jnp.int32)[:, None]) & keep[
        None, :
    ]


def land_blocks(total, block_index, valid, incoming):
    return total.at[block_index].add(jnp.where(valid[:, None, None], incoming, 0.0))


def shards(node_features, tiles, tile_list, weight, texts, selected, pairing):
    groups = lax.axis_size(GRP)
    members = lax.axis_size(DEV)
    grp_index = lax.axis_index(GRP)
    dev_index = lax.axis_index(DEV)
    device = grp_index * members + dev_index
    block_rows = tiles.shape[1]
    feat_width = node_features.shape[1]
    blocks_dev = node_features.shape[0] // block_rows
    tile_dev = tiles.shape[0]
    sel_dev = selected.shape[0]
    capacity = CAP
    total_sel = sel_dev * groups * members
    rounded = node_features.astype(jnp.bfloat16).reshape(blocks_dev, block_rows, feat_width)
    my_list = lax.dynamic_slice_in_dim(tile_list, device * tile_dev, tile_dev, 0)
    row_block = my_list[:, 0] - device * blocks_dev
    col_owner = my_list[:, 1] // blocks_dev
    col_block = my_list[:, 1] - col_owner * blocks_dev
    owner_grp = col_owner // members
    owner_dev = col_owner % members
    is_local = col_owner == device
    is_near = (owner_grp == grp_index) & jnp.logical_not(is_local)
    is_far = (owner_dev == dev_index) & (owner_grp != grp_index)
    positions = jnp.arange(tile_dev, dtype=jnp.int32)
    earlier = (col_owner[:, None] == col_owner[None, :]) & (positions[None, :] < positions[:, None])
    slot_rank = jnp.sum(earlier.astype(jnp.int32), axis=1)
    near_slot = owner_dev * capacity + slot_rank
    far_slot = owner_grp * capacity + slot_rank
    group_lists = lax.dynamic_slice_in_dim(
        tile_list, grp_index * members * tile_dev, members * tile_dev, 0
    ).reshape(members, tile_dev, 2)
    near_peers = grp_index * members + jnp.arange(members, dtype=jnp.int32)
    near_index, near_valid = slot_plan(group_lists, near_peers, device, blocks_dev, capacity)
    far_lists = lax.dynamic_index_in_dim(
        tile_list.reshape(groups, members, tile_dev, 2), dev_index, 1, False
    )
    far_peers = jnp.arange(groups, dtype=jnp.int32) * members + dev_index
    far_index, far_valid = slot_plan(far_lists, far_peers, device, blocks_dev, capacity)
    zero_half = jnp.zeros((), jnp.bfloat16)
    sel_local = selected - device * blocks_dev * block_rows
    sel_block = sel_local // block_rows
    sel_offset = sel_local % block_rows
    picked = jnp.take(tiles, sel_offset, axis=1)
    tile_rows = jnp.where((row_block[:, None] == sel_block[None, :])[:, :, None], picked, zero_half)
    near_pick = slot_pick(near_slot, is_near, members * capacity)
    far_pick = slot_pick(far_slot, is_far, groups * capacity)
    near_rows = jnp.einsum(
        "st,tkc->skc", near_pick.astype(jnp.bfloat16), tile_rows, preferred_element_type=jnp.float32
    ).astype(jnp.bfloat16)
    far_rows = jnp.einsum(
        "st,tkc->skc", far_pick.astype(jnp.bfloat16), tile_rows, preferred_element_type=jnp.float32
    ).astype(jnp.bfloat16)
    local_tile_rows = jnp.where(is_local[:, None, None], tile_rows, zero_half)
    local_sources = jnp.take(rounded, col_block, axis=0)
    messages = jnp.einsum(
        "tkc,tcd->kd", local_tile_rows, local_sources, preferred_element_type=jnp.float32
    )
    near_fwd_in = lax.all_to_all(
        near_rows.reshape(members, capacity, sel_dev, block_rows),
        DEV,
        split_axis=0,
        concat_axis=0,
        tiled=True,
    )
    near_own = jnp.take(rounded, near_index, axis=0).reshape(
        members, capacity, block_rows, feat_width
    )
    near_part = jnp.einsum(
        "pqkc,pqcd->pkd", near_fwd_in, near_own, preferred_element_type=jnp.float32
    )
    near_back = lax.all_to_all(near_part, DEV, split_axis=0, concat_axis=0, tiled=True)
    far_fwd_in = lax.all_to_all(
        far_rows.reshape(groups, capacity, sel_dev, block_rows),
        GRP,
        split_axis=0,
        concat_axis=0,
        tiled=True,
    )
    far_own = jnp.take(rounded, far_index, axis=0).reshape(groups, capacity, block_rows, feat_width)
    far_part = jnp.einsum("pqkc,pqcd->pkd", far_fwd_in, far_own, preferred_element_type=jnp.float32)
    far_back = lax.all_to_all(far_part, GRP, split_axis=0, concat_axis=0, tiled=True)
    messages = messages + jnp.sum(near_back, axis=0) + jnp.sum(far_back, axis=0)
    chosen = node_features[sel_local] + messages
    before = jnp.dot(chosen, weight, precision=PRECISE)
    hidden = gelu_value(before)
    node_norm = jnp.sqrt(jnp.sum(hidden * hidden, axis=1, keepdims=True) + EPS)
    unit_nodes = hidden / node_norm
    text_norm = jnp.sqrt(jnp.sum(texts * texts, axis=1, keepdims=True) + EPS)
    unit_texts = texts / text_norm
    node_rows, pair_rows = (gather_directly(unit_nodes, DEV, 0), gather_directly(pairing, DEV, 0))
    text_cols = gather_directly(unit_texts, GRP, 0)
    scores = SCALE * lax.dot_general(
        node_rows, text_cols, (((1,), (1,)), ((), ())), precision=PRECISE
    )
    exp_scores = jnp.exp(scores)
    row_total = over_axes(jnp.sum(exp_scores, axis=1), DEV)
    col_total = over_copies(jnp.sum(exp_scores, axis=0), GRP)
    col_global = (
        (jnp.arange(groups, dtype=jnp.int32)[:, None] * members + dev_index) * sel_dev
        + jnp.arange(sel_dev, dtype=jnp.int32)[None, :]
    ).reshape(-1)
    target = pair_rows[:, None] == col_global[None, :]
    score_grads = 0.5 * (
        exp_scores / row_total[:, None] + exp_scores / col_total[None, :]
    ) - target.astype(jnp.float32)
    node_part = SCALE * jnp.dot(score_grads, text_cols, precision=PRECISE)
    node_dir = summed_on_arrival(node_part, DEV, 0)
    text_part = SCALE * lax.dot_general(
        score_grads, node_rows, (((0,), (0,)), ((), ())), precision=PRECISE
    )
    text_dir = summed_on_arrival(text_part, GRP, 0)
    own_rows = lax.dynamic_slice_in_dim(row_total, dev_index * sel_dev, sel_dev, 0)
    own_cols = lax.dynamic_slice_in_dim(col_total, grp_index * sel_dev, sel_dev, 0)
    positive = jnp.sum(jnp.where(target, scores, 0.0))
    lse_sum, pos_sum = (
        over_axes(jnp.sum(jnp.log(own_rows)) + jnp.sum(jnp.log(own_cols)), GRP_DEV),
        over_axes(positive, GRP_DEV),
    )
    contrast_loss = lse_sum / (2.0 * total_sel) - pos_sum / total_sel
    node_back = (
        node_dir - unit_nodes * jnp.sum(unit_nodes * node_dir, axis=1, keepdims=True)
    ) / node_norm
    grad_texts = (
        text_dir - unit_texts * jnp.sum(unit_texts * text_dir, axis=1, keepdims=True)
    ) / text_norm
    pre_grad = node_back * gelu_slope(before)
    weight_term = lax.dot_general(chosen, pre_grad, (((0,), (0,)), ((), ())), precision=PRECISE)
    grad_weight = lax.psum(weight_term, GRP_DEV)
    row_grads = lax.dot_general(pre_grad, weight, (((1,), (1,)), ((), ())), precision=PRECISE)
    rounded_grads = row_grads.astype(jnp.bfloat16)
    empty_blocks = jnp.zeros((blocks_dev, block_rows, feat_width), jnp.float32)
    local_spread = jnp.einsum(
        "tkc,kd->tcd", local_tile_rows, rounded_grads, preferred_element_type=jnp.float32
    )
    grad_blocks = empty_blocks.at[col_block].add(local_spread)
    near_rows_in = lax.all_to_all(
        near_rows.reshape(members, capacity, sel_dev, block_rows),
        DEV,
        split_axis=0,
        concat_axis=0,
        tiled=True,
    )
    near_grads_in = gather_directly(rounded_grads, DEV, 0).reshape(members, sel_dev, feat_width)
    near_spread = jnp.einsum(
        "pqkc,pkd->pqcd", near_rows_in, near_grads_in, preferred_element_type=jnp.float32
    )
    grad_blocks = land_blocks(
        grad_blocks, near_index, near_valid, near_spread.reshape(-1, block_rows, feat_width)
    )
    far_rows_in = lax.all_to_all(
        far_rows.reshape(groups, capacity, sel_dev, block_rows),
        GRP,
        split_axis=0,
        concat_axis=0,
        tiled=True,
    )
    far_grads_in = gather_directly(rounded_grads, GRP, 0).reshape(groups, sel_dev, feat_width)
    far_spread = jnp.einsum(
        "pqkc,pkd->pqcd", far_rows_in, far_grads_in, preferred_element_type=jnp.float32
    )
    grad_blocks = land_blocks(
        grad_blocks, far_index, far_valid, far_spread.reshape(-1, block_rows, feat_width)
    )
    grad_nodes = grad_blocks.reshape(-1, feat_width).at[sel_local].add(row_grads)
    return (contrast_loss, grad_nodes, grad_weight, grad_texts)


def solution(mesh):
    finer = Mesh(mesh.devices.reshape(4, 2, 4, 4), ("grp_0", "grp_1", "dev_0", "dev_1"))
    placed = (
        P(GRP_DEV, None),
        P(GRP_DEV, None, None),
        P(),
        P(),
        P(GRP_DEV, None),
        P(GRP_DEV),
        P(GRP_DEV),
    )
    return jax.shard_map(
        shards,
        mesh=finer,
        in_specs=placed,
        out_specs=(P(), P(GRP_DEV, None), P(), P(GRP_DEV, None)),
        check_vma=False,
    )
```

profile of v0, /device:TPU:1, one launch (start us, length us, event | category | flops | bytes accessed | tf_op | source)
XLA Modules:
  0.0 436.1 jit_solution(10875609758458109484)
XLA Ops:
  14.9 5.8 %all-to-all-start.2 = ((bf16[8,2,32,128]{3,2,1,0:T(8,128)(2,1)}), bf16[8,2,32,128]{3,2,1,0:T(8,128)(2,1)S(1)}, u32[]{:S(2)}, u32[]{:S(2)}) async-start(bf16[8,2,32,128]{3,2,1,0:T(8,128)(2,1)} %copy.34), calls=%async_computation.2 | async-start | bytes 262144 | tf_op jit(solution)/shard_map/all_to_all | solution.py:162
  34.2 7.8 %all-to-all-start = ((bf16[16,2,32,128]{3,2,1,0:T(8,128)(2,1)}), bf16[16,2,32,128]{3,2,1,0:T(8,128)(2,1)S(1)}, u32[]{:S(2)}, u32[]{:S(2)}) async-start(bf16[16,2,32,128]{3,2,1,0:T(8,128)(2,1)} %copy.30), calls=%async_computation | async-start | bytes 524288 | tf_op jit(solution)/shard_map/all_to_all | solution.py:148
  49.8 6.1 %all-to-all-start.3 = ((f32[8,32,768]{2,1,0:T(8,128)}), f32[8,32,768]{2,1,0:T(8,128)}, u32[]{:S(2)}, u32[]{:S(2)}) async-start(f32[8,32,768]{2,1,0:T(8,128)} %fusion.15), calls=%async_computation.3 | async-start | bytes 1572864 | tf_op jit(solution)/shard_map/all_to_all | solution.py:171
  56.0 5.1 %fusion.12 = f32[16,32,768]{2,1,0:T(8,128)} fusion(bf16[16,2,32,128]{3,2,1,0:T(8,128)(2,1)S(1)} %all-to-all-done, bf16[16,2,128,768]{3,2,1,0:T(8,128)(2,1)} %bitcast.98, pred[16,2]{1,0:T(8,128)(4,1)S(1)} %copy.31), kind=kOutput, calls=%fused_computation.24 | convolution fusion | flops 204472320 | bytes 8126496 | tf_op jit(solution)/shard_map/pqkc,pqcd->pkd/dot_general | solution.py:158
  61.1 7.2 %all-to-all-done.3 = f32[8,32,768]{2,1,0:T(8,128)} async-done(((f32[8,32,768]{2,1,0:T(8,128)}), f32[8,32,768]{2,1,0:T(8,128)}, u32[]{:S(2)}, u32[]{:S(2)}) %all-to-all-start.3) | async-done | bytes 786464 | tf_op jit(solution)/shard_map/all_to_all | solution.py:171
  68.2 4.4 %all-to-all-start.1 = ((f32[16,32,768]{2,1,0:T(8,128)}), f32[16,32,768]{2,1,0:T(8,128)}, u32[]{:S(2)}, u32[]{:S(2)}) async-start(f32[16,32,768]{2,1,0:T(8,128)} %fusion.12), calls=%async_computation.1 | async-start | bytes 3145728 | tf_op jit(solution)/shard_map/all_to_all | solution.py:161
  74.8 6.6 %gather_fusion.2 = bf16[52,128,768]{2,1,0:T(8,128)(2,1)} fusion(bf16[4,128,768]{2,1,0:T(8,128)(2,1)S(1)} %bitcast.97, s32[1024]{0:T(1024)S(1)} %pad_clamp_fusion.2), kind=kCustom, calls=%fused_computation.2 | custom fusion | bytes 20447440 | tf_op jit(solution)/shard_map/jit(_take)/gather | solution.py:144
  82.8 10.6 %all-to-all-done.1 = f32[16,32,768]{2,1,0:T(8,128)} async-done(((f32[16,32,768]{2,1,0:T(8,128)}), f32[16,32,768]{2,1,0:T(8,128)}, u32[]{:S(2)}, u32[]{:S(2)}) %all-to-all-start.1) | async-done | bytes 1572896 | tf_op jit(solution)/shard_map/all_to_all | solution.py:161
  94.0 5.3 %all-to-all-start.7 = ((s32[16,1,32]{2,1,0:T(1,128)}), s32[16,1,32]{2,1,0:T(1,128)S(1)}, u32[]{:S(2)}, u32[]{:S(2)}) async-start(s32[16,1,32]{2,1,0:T(1,128)} %broadcast_in_dim.206), calls=%async_computation.7 | async-start | bytes 16384 | tf_op jit(solution)/shard_map/all_to_all | solution.py:30
  100.9 5.1 %fusion.27 = f32[32,768]{1,0:T(8,128)S(1)} fusion(f32[32,768]{1,0:T(8,128)S(1)} %gather_fusion, f32[32,768]{1,0:T(8,128)S(1)} %reduce_sum.157, f32[32,768]{1,0:T(8,128)S(1)} %reduce_sum.155, bf16[52,128,768]{2,1,0:T(8,128)(2,1)} %gather_fusion.2, pred[52]{0:T(512)(128)(4,1)} %get-tuple-element.15, bf16[52,32,128]{2,1,0:T(8,128)(2,1)} %copy-done.2, ...), kind=kOutput, calls=%fused_computation.33 | convolution fusion | flops 332554240 | bytes 11042920 | tf_op jit(solution)/shard_map/tkc,tcd->kd/dot_general | solution.py:145
  106.9 6.8 %all-to-all-start.5 = ((f32[8,32,768]{2,1,0:T(8,128)}), f32[8,32,768]{2,1,0:T(8,128)S(1)}, u32[]{:S(2)}, u32[]{:S(2)}) async-start(f32[8,32,768]{2,1,0:T(8,128)} %broadcast_in_dim.204), calls=%async_computation.5 | async-start | bytes 1572864 | tf_op jit(solution)/shard_map/all_to_all | solution.py:30
  115.4 10.7 %all-to-all-done.5 = f32[8,32,768]{2,1,0:T(8,128)S(1)} async-done(((f32[8,32,768]{2,1,0:T(8,128)}), f32[8,32,768]{2,1,0:T(8,128)S(1)}, u32[]{:S(2)}, u32[]{:S(2)}) %all-to-all-start.5) | async-done | bytes 786464 | tf_op jit(solution)/shard_map/all_to_all | solution.py:30
  127.5 6.3 %all-to-all-start.4 = ((f32[16,32,768]{2,1,0:T(8,128)}), f32[16,32,768]{2,1,0:T(8,128)}, u32[]{:S(2)}, u32[]{:S(2)}) async-start(f32[16,32,768]{2,1,0:T(8,128)} %broadcast_in_dim.203), calls=%async_computation.4 | async-start | bytes 3145728 | tf_op jit(solution)/shard_map/all_to_all | solution.py:30
  135.2 19.2 %all-to-all-done.4 = f32[16,32,768]{2,1,0:T(8,128)} async-done(((f32[16,32,768]{2,1,0:T(8,128)}), f32[16,32,768]{2,1,0:T(8,128)}, u32[]{:S(2)}, u32[]{:S(2)}) %all-to-all-start.4) | async-done | bytes 1572896 | tf_op jit(solution)/shard_map/all_to_all | solution.py:30
  159.2 7.4 %all-to-all-start.6 = ((f32[8,1,256]{2,1,0:T(1,128)}), f32[8,1,256]{2,1,0:T(1,128)S(1)}, u32[]{:S(2)}, u32[]{:S(2)}) async-start(f32[8,1,256]{2,1,0:T(1,128)} %broadcast_in_dim.205), calls=%async_computation.6 | async-start | bytes 16384 | tf_op jit(solution)/shard_map/all_to_all | solution.py:30
  166.7 6.5 %psum.77 = f32[512]{0:T(512)S(1)} all-reduce(f32[512]{0:T(512)S(1)} %get-tuple-element.6), channel_id=1, replica_groups=mesh['grp_0'=4,'grp_1'=2,'dev_0'=4,'dev_1'=4] {'dev_0'}, use_global_device_ids=true, to_apply=%region_10.11 | all-reduce | flops 512 | bytes 4096 | tf_op jit(solution)/shard_map/psum | solution.py:38
  173.2 6.3 %psum.78 = f32[512]{0:T(512)S(1)} all-reduce(f32[512]{0:T(512)S(1)} %psum.77), channel_id=1, replica_groups=mesh['grp_0'=4,'grp_1'=2,'dev_0'=4,'dev_1'=4] {'dev_1'}, use_global_device_ids=true, to_apply=%region_11.12 | all-reduce | flops 512 | bytes 4096 | tf_op jit(solution)/shard_map/psum | solution.py:38
  183.7 8.9 %all-to-all-start.11 = ((f32[8,32,768]{2,1,0:T(8,128)}), f32[8,32,768]{2,1,0:T(8,128)S(1)}, u32[]{:S(2)}, u32[]{:S(2)}) async-start(f32[8,32,768]{2,1,0:T(8,128)} %bitcast.104), calls=%async_computation.11 | async-start | bytes 1572864 | tf_op jit(solution)/shard_map/all_to_all | solution.py:53
  196.6 8.3 %all-to-all-done.11 = f32[8,32,768]{2,1,0:T(8,128)S(1)} async-done(((f32[8,32,768]{2,1,0:T(8,128)}), f32[8,32,768]{2,1,0:T(8,128)S(1)}, u32[]{:S(2)}, u32[]{:S(2)}) %all-to-all-start.11) | async-done | bytes 786464 | tf_op jit(solution)/shard_map/all_to_all | solution.py:53
  213.6 8.3 %all-reduce.2 = (f32[]{:T(128)}, f32[]{:T(128)}) all-reduce(f32[]{:T(128)S(6)} %add.315, f32[]{:T(128)} %get-tuple-element.4), channel_id=1, replica_groups=mesh['grp_0'=4,'grp_1'=2,'dev_0'=4,'dev_1'=4] {'grp_0'}, use_global_device_ids=true, to_apply=%region_16.17 | all-reduce | flops 2 | bytes 16 | tf_op jit(solution)/shard_map/psum | solution.py:38
  221.9 4.8 %all-reduce.3 = (f32[]{:T(128)}, f32[]{:T(128)}) all-reduce(f32[]{:T(128)} %get-tuple-element.11, f32[]{:T(128)} %get-tuple-element.12), channel_id=1, replica_groups=mesh['grp_0'=4,'grp_1'=2,'dev_0'=4,'dev_1'=4] {'grp_1'}, use_global_device_ids=true, to_apply=%region_17.18 | all-reduce | flops 2 | bytes 16 | tf_op jit(solution)/shard_map/psum | solution.py:38
  226.8 9.4 %all-reduce.1 = (f32[]{:T(128)}, f32[]{:T(128)}) all-reduce(f32[]{:T(128)} %get-tuple-element.13, f32[]{:T(128)} %get-tuple-element.14), channel_id=1, replica_groups=mesh['grp_0'=4,'grp_1'=2,'dev_0'=4,'dev_1'=4] {'dev_0'}, use_global_device_ids=true, to_apply=%region_18.19 | all-reduce | flops 2 | bytes 16 | tf_op jit(solution)/shard_map/psum | solution.py:38
  236.1 9.0 %all-reduce = (f32[]{:T(128)}, f32[]{:T(128)}) all-reduce(f32[]{:T(128)} %get-tuple-element.9, f32[]{:T(128)} %get-tuple-element.10), channel_id=1, replica_groups=mesh['grp_0'=4,'grp_1'=2,'dev_0'=4,'dev_1'=4] {'dev_1'}, use_global_device_ids=true, to_apply=%region_19.20 | all-reduce | flops 2 | bytes 16 | tf_op jit(solution)/shard_map/psum | solution.py:38
  253.4 7.7 %all-to-all-start.10 = ((bf16[8,32,768]{2,1,0:T(8,128)(2,1)}), bf16[8,32,768]{2,1,0:T(8,128)(2,1)S(1)}, u32[]{:S(2)}, u32[]{:S(2)}) async-start(bf16[8,32,768]{2,1,0:T(8,128)(2,1)} %broadcast_in_dim.215), calls=%async_computation.10 | async-start | bytes 786432 | tf_op jit(solution)/shard_map/all_to_all | solution.py:30
  261.2 8.7 %fusion.38 = f32[52,128,768]{2,1,0:T(8,128)} fusion(bf16[52,32,128]{2,1,0:T(8,128)(2,1)S(1)} %copy-done.3, pred[52]{0:T(512)(128)(4,1)S(1)} %copy-done.30, bf16[32,768]{1,0:T(8,128)(2,1)S(1)} %get-tuple-element.37), kind=kOutput, calls=%fused_computation.48 | convolution fusion | flops 327368704 | bytes 20922420 | tf_op jit(solution)/shard_map/tkc,kd->tcd/dot_general | solution.py:222
  274.7 46.8 %scatter_fusion = f32[4,128,768]{2,1,0:T(8,128)} fusion(f32[4,128,768]{2,1,0:T(8,128)} %broadcast_in_dim.208, s32[52]{0:T(128)S(1)} %bitcast.109, f32[52,128,768]{2,1,0:T(8,128)} %fusion.38), kind=kCustom, calls=%fused_computation.5 | custom fusion | flops 5111808 | bytes 61341904 | tf_op jit(solution)/shard_map/scatter-add | solution.py:225
  330.5 8.4 %all-to-all-done.9 = bf16[16,32,768]{2,1,0:T(8,128)(2,1)S(1)} async-done(((bf16[16,32,768]{2,1,0:T(8,128)(2,1)}), bf16[16,32,768]{2,1,0:T(8,128)(2,1)S(1)}, u32[]{:S(2)}, u32[]{:S(2)}) %all-to-all-start.9) | async-done | bytes 786464 | tf_op jit(solution)/shard_map/all_to_all | solution.py:30
  338.9 6.4 %fusion.30 = f32[16,2,128,768]{3,2,1,0:T(8,128)} fusion(bf16[16,2,32,128]{3,2,1,0:T(8,128)(2,1)S(1)} %copy-done.7, bf16[16,32,768]{2,1,0:T(8,128)(2,1)S(1)} %all-to-all-done.9), kind=kOutput, calls=%fused_computation.34 | convolution fusion | flops 201326592 | bytes 13631488 | tf_op jit(solution)/shard_map/pqkc,pkd->pqcd/dot_general | solution.py:234
  345.3 10.9 %bitcast_select_fusion = f32[32,128,768]{2,1,0:T(8,128)} fusion(f32[16,2,128,768]{3,2,1,0:T(8,128)} %fusion.30, pred[32]{0:T(512)(128)(4,1)S(1)} %copy-done.28), kind=kLoop, calls=%fused_computation.9 | loop fusion | flops 3145728 | bytes 25165856 | tf_op jit(solution)/shard_map/jit(_where)/select_n | solution.py:88
  356.2 28.6 %scatter_fusion.1 = f32[4,128,768]{2,1,0:T(8,128)} fusion(f32[4,128,768]{2,1,0:T(8,128)} %scatter_fusion, s32[32]{0:T(128)S(1)} %copy-done.27, f32[32,128,768]{2,1,0:T(8,128)} %bitcast_select_fusion), kind=kCustom, calls=%fused_computation.6 | custom fusion | flops 3145728 | bytes 37748864 | tf_op jit(solution)/shard_map/scatter-add | solution.py:88
  384.8 14.6 %scatter_fusion.2 = f32[4,128,768]{2,1,0:T(8,128)} fusion(f32[4,128,768]{2,1,0:T(8,128)} %scatter_fusion.1, s32[16]{0:T(128)S(1)} %copy-done.25, f32[16,128,768]{2,1,0:T(8,128)} %bitcast_select_fusion.1), kind=kCustom, calls=%fused_computation.7 | custom fusion | flops 1572864 | bytes 18874432 | tf_op jit(solution)/shard_map/scatter-add | solution.py:88
  402.9 22.0 %all-reduce.6.cloned.1.call-done = f32[768,768]{1,0:T(8,128)} async-done(((f32[768,768]{1,0:T(8,128)}), f32[768,768]{1,0:T(8,128)}) %all-reduce.6.cloned.1.call-update) | async-done | bytes 2359312 | tf_op jit(solution)/shard_map/psum | solution.py:218
  (172 shorter events, 88.0 us)
Async XLA Ops:
  7.2 106.6 %copy-start = (f32[768,768]{1,0:T(8,128)S(1)}, f32[768,768]{1,0:T(8,128)}, u32[]{:S(2)}) copy-start(f32[768,768]{1,0:T(8,128)} %param.10) | copy-start | bytes 7077892
  7.2 13.5 %copy-start.10 = (s32[6656,2]{0,1:T(2,128)S(1)}, s32[6656,2]{0,1:T(2,128)}, u32[]{:S(2)}) copy-start(s32[6656,2]{0,1:T(2,128)} %param.9) | copy-start | bytes 159748
  14.9 19.2 %all-to-all-start.2 = ((bf16[8,2,32,128]{3,2,1,0:T(8,128)(2,1)}), bf16[8,2,32,128]{3,2,1,0:T(8,128)(2,1)S(1)}, u32[]{:S(2)}, u32[]{:S(2)}) async-start(bf16[8,2,32,128]{3,2,1,0:T(8,128)(2,1)} %copy.34), calls=%async_computation.2 | async-start | bytes 262144 | tf_op jit(solution)/shard_map/all_to_all | solution.py:162
  34.2 15.6 %copy-start.8 = (bf16[8,2,32,128]{3,2,1,0:T(8,128)(2,1)}, bf16[8,2,32,128]{3,2,1,0:T(8,128)(2,1)S(1)}, u32[]{:S(2)}) copy-start(bf16[8,2,32,128]{3,2,1,0:T(8,128)(2,1)S(1)} %all-to-all-done.2) | copy-start | bytes 393220
  34.2 15.6 %all-to-all-start = ((bf16[16,2,32,128]{3,2,1,0:T(8,128)(2,1)}), bf16[16,2,32,128]{3,2,1,0:T(8,128)(2,1)S(1)}, u32[]{:S(2)}, u32[]{:S(2)}) async-start(bf16[16,2,32,128]{3,2,1,0:T(8,128)(2,1)} %copy.30), calls=%async_computation | async-start | bytes 524288 | tf_op jit(solution)/shard_map/all_to_all | solution.py:148
  41.9 13.9 %copy-start.23 = (s32[16,2]{0,1:T(2,128)S(1)}, s32[16,2]{0,1:T(2,128)}, u32[]{:S(2)}) copy-start(s32[16,2]{0,1:T(2,128)} %copy-done.22) | copy-start | bytes 388
  49.8 18.5 %all-to-all-start.3 = ((f32[8,32,768]{2,1,0:T(8,128)}), f32[8,32,768]{2,1,0:T(8,128)}, u32[]{:S(2)}, u32[]{:S(2)}) async-start(f32[8,32,768]{2,1,0:T(8,128)} %fusion.15), calls=%async_computation.3 | async-start | bytes 1572864 | tf_op jit(solution)/shard_map/all_to_all | solution.py:171
  61.1 13.7 %copy-start.17 = (s32[52,1]{0,1:T(1,128)S(1)}, s32[52,1]{0,1:T(1,128)}, u32[]{:S(2)}) copy-start(s32[52,1]{0,1:T(1,128)} %get-tuple-element.16) | copy-start | bytes 628
  68.2 25.2 %all-to-all-start.1 = ((f32[16,32,768]{2,1,0:T(8,128)}), f32[16,32,768]{2,1,0:T(8,128)}, u32[]{:S(2)}, u32[]{:S(2)}) async-start(f32[16,32,768]{2,1,0:T(8,128)} %fusion.12), calls=%async_computation.1 | async-start | bytes 3145728 | tf_op jit(solution)/shard_map/all_to_all | solution.py:161
  74.8 18.6 %copy-start.32 = (s32[32]{0:T(128)S(1)}, s32[32]{0:T(128)}, u32[]{:S(2)}) copy-start(s32[32]{0:T(128)} %param.13) | copy-start | bytes 388
  74.8 26.1 %copy-start.29 = (pred[52]{0:T(512)(128)(4,1)S(1)}, pred[52]{0:T(512)(128)(4,1)}, u32[]{:S(2)}) copy-start(pred[52]{0:T(512)(128)(4,1)} %get-tuple-element.21) | copy-start | bytes 160
  81.5 19.4 %copy-start.19 = (f32[32]{0:T(128)}, f32[32]{0:T(128)S(1)}, u32[]{:S(2)}) copy-start(f32[32]{0:T(128)S(1)} %add_sqrt_fusion) | copy-start | bytes 388
  94.0 12.0 %all-to-all-start.7 = ((s32[16,1,32]{2,1,0:T(1,128)}), s32[16,1,32]{2,1,0:T(1,128)S(1)}, u32[]{:S(2)}, u32[]{:S(2)}) async-start(s32[16,1,32]{2,1,0:T(1,128)} %broadcast_in_dim.206), calls=%async_computation.7 | async-start | bytes 16384 | tf_op jit(solution)/shard_map/all_to_all | solution.py:30
  106.9 19.1 %all-to-all-start.5 = ((f32[8,32,768]{2,1,0:T(8,128)}), f32[8,32,768]{2,1,0:T(8,128)S(1)}, u32[]{:S(2)}, u32[]{:S(2)}) async-start(f32[8,32,768]{2,1,0:T(8,128)} %broadcast_in_dim.204), calls=%async_computation.5 | async-start | bytes 1572864 | tf_op jit(solution)/shard_map/all_to_all | solution.py:30
  126.1 32.6 %copy-start.4 = (f32[8,32,768]{2,1,0:T(8,128)}, f32[8,32,768]{2,1,0:T(8,128)S(1)}, u32[]{:S(2)}) copy-start(f32[8,32,768]{2,1,0:T(8,128)S(1)} %all-to-all-done.5) | copy-start | bytes 2359300
  127.5 26.9 %all-to-all-start.4 = ((f32[16,32,768]{2,1,0:T(8,128)}), f32[16,32,768]{2,1,0:T(8,128)}, u32[]{:S(2)}, u32[]{:S(2)}) async-start(f32[16,32,768]{2,1,0:T(8,128)} %broadcast_in_dim.203), calls=%async_computation.4 | async-start | bytes 3145728 | tf_op jit(solution)/shard_map/all_to_all | solution.py:30
  159.2 20.2 %all-to-all-start.6 = ((f32[8,1,256]{2,1,0:T(1,128)}), f32[8,1,256]{2,1,0:T(1,128)S(1)}, u32[]{:S(2)}, u32[]{:S(2)}) async-start(f32[8,1,256]{2,1,0:T(1,128)} %broadcast_in_dim.205), calls=%async_computation.6 | async-start | bytes 16384 | tf_op jit(solution)/shard_map/all_to_all | solution.py:30
  183.7 21.2 %all-to-all-start.11 = ((f32[8,32,768]{2,1,0:T(8,128)}), f32[8,32,768]{2,1,0:T(8,128)S(1)}, u32[]{:S(2)}, u32[]{:S(2)}) async-start(f32[8,32,768]{2,1,0:T(8,128)} %bitcast.104), calls=%async_computation.11 | async-start | bytes 1572864 | tf_op jit(solution)/shard_map/all_to_all | solution.py:53
  192.5 16.7 %copy-start.14 = (pred[16,52]{1,0:T(8,128)(4,1)S(1)}, pred[16,52]{1,0:T(8,128)(4,1)}, u32[]{:S(2)}) copy-start(pred[16,52]{1,0:T(8,128)(4,1)} %copy-done.13) | copy-start | bytes 2500
  192.5 17.5 %copy-start.16 = (pred[8,52]{1,0:T(8,128)(4,1)S(1)}, pred[8,52]{1,0:T(8,128)(4,1)}, u32[]{:S(2)}) copy-start(pred[8,52]{1,0:T(8,128)(4,1)} %copy-done.15) | copy-start | bytes 1252
  204.8 43.9 %all-to-all-start.8 = ((f32[16,32,768]{2,1,0:T(8,128)}), f32[16,32,768]{2,1,0:T(8,128)}, u32[]{:S(2)}, u32[]{:S(2)}) async-start(f32[16,32,768]{2,1,0:T(8,128)} %bitcast.102), calls=%async_computation.8 | async-start | bytes 3145728 | tf_op jit(solution)/shard_map/all_to_all | solution.py:53
  246.5 14.7 %copy-start.3 = (bf16[52,32,128]{2,1,0:T(8,128)(2,1)S(1)}, bf16[52,32,128]{2,1,0:T(8,128)(2,1)}, u32[]{:S(2)}) copy-start(bf16[52,32,128]{2,1,0:T(8,128)(2,1)} %copy-done.2) | copy-start | bytes 1277956
  246.5 14.7 %copy-start.30 = (pred[52]{0:T(512)(128)(4,1)S(1)}, pred[52]{0:T(512)(128)(4,1)}, u32[]{:S(2)}) copy-start(pred[52]{0:T(512)(128)(4,1)} %get-tuple-element.21) | copy-start | bytes 160
  253.4 68.0 %all-to-all-start.10 = ((bf16[8,32,768]{2,1,0:T(8,128)(2,1)}), bf16[8,32,768]{2,1,0:T(8,128)(2,1)S(1)}, u32[]{:S(2)}, u32[]{:S(2)}) async-start(bf16[8,32,768]{2,1,0:T(8,128)(2,1)} %broadcast_in_dim.215), calls=%async_computation.10 | async-start | bytes 786432 | tf_op jit(solution)/shard_map/all_to_all | solution.py:30
  261.2 163.8 %all-reduce.6.cloned.1.call-start = ((), (), s32[]{:S(2)}) async-start(), calls=%async_computation.12 | async-start | bytes 4718592 | tf_op jit(solution)/shard_map/psum | solution.py:218
  274.7 51.4 %copy-start.9 = (bf16[8,2,32,128]{3,2,1,0:T(8,128)(2,1)S(1)}, bf16[8,2,32,128]{3,2,1,0:T(8,128)(2,1)}, u32[]{:S(2)}) copy-start(bf16[8,2,32,128]{3,2,1,0:T(8,128)(2,1)} %copy-done.8) | copy-start | bytes 393220
  322.4 16.5 %all-to-all-start.9 = ((bf16[16,32,768]{2,1,0:T(8,128)(2,1)}), bf16[16,32,768]{2,1,0:T(8,128)(2,1)S(1)}, u32[]{:S(2)}, u32[]{:S(2)}) async-start(bf16[16,32,768]{2,1,0:T(8,128)(2,1)} %broadcast_in_dim.211), calls=%async_computation.9 | async-start | bytes 1572864 | tf_op jit(solution)/shard_map/all_to_all | solution.py:30
  327.1 11.9 %copy-start.7 = (bf16[16,2,32,128]{3,2,1,0:T(8,128)(2,1)S(1)}, bf16[16,2,32,128]{3,2,1,0:T(8,128)(2,1)}, u32[]{:S(2)}) copy-start(bf16[16,2,32,128]{3,2,1,0:T(8,128)(2,1)} %copy-done.6) | copy-start | bytes 786436
  330.5 14.8 %copy-start.28 = (pred[32]{0:T(512)(128)(4,1)S(1)}, pred[32]{0:T(512)(128)(4,1)}, u32[]{:S(2)}) copy-start(pred[32]{0:T(512)(128)(4,1)} %broadcast_in_dim.209) | copy-start | bytes 100
  356.2 28.6 %copy-start.25 = (s32[16]{0:T(128)S(1)}, s32[16]{0:T(128)}, u32[]{:S(2)}) copy-start(s32[16]{0:T(128)} %copy-done.24) | copy-start | bytes 196
  384.8 14.6 %copy-start.21 = (s32[32]{0:T(128)S(1)}, s32[32]{0:T(128)}, u32[]{:S(2)}) copy-start(s32[32]{0:T(128)} %get-tuple-element.33) | copy-start | bytes 388
  399.4 28.8 %copy-start.1 = (f32[768,768]{1,0:T(8,128)S(1)}, f32[768,768]{1,0:T(8,128)}, u32[]{:S(2)}) copy-start(f32[768,768]{1,0:T(8,128)} %param.10) | copy-start | bytes 7077892
  (14 other events, 75.6 us)
Sparse Core Ops, SparseCore 0:
  273.5 151.3 all-reduce.5
where the time goes:
time: 438 us; the launch traced here: 436 us
  other arithmetic  123 us (28%)
  waiting for transfers between devices  90.7 us (21%)
  starting transfers between devices  74.5 us (17%)
  matrix products  50.8 us (12%)
  blocking collectives  44.3 us (10%)
  local copies, waits for them, and re-layouts  34.1 us (8%)
  between operations  18.3 us (4%)
    scatter-add x1, other arithmetic, shards(): grad_blocks = empty_blocks.at[col_block].add(local_spread)  46.8 us
    psum x6, blocking collectives, over_axes(): return functools.reduce(lax.psum, axes, array)  44.3 us
    scatter-add x2, other arithmetic, land_blocks(): total.at[block_index].add(jnp.where(valid[:, None, None], incoming, 0.0))  43.2 us
    all_to_all x6, waiting for transfers between devices, from_everyone(): return lax.all_to_all(copies, axis, split_axis=0, concat_axis=0, tiled=True)  38.2 us
    all_to_all x6, starting transfers between devices, from_everyone(): return lax.all_to_all(copies, axis, split_axis=0, concat_axis=0, tiled=True)  37.2 us
    psum x1, waiting for transfers between devices, shards(): grad_weight = lax.psum(weight_term, GRP_DEV)  22 us
    select_n x2, other arithmetic, land_blocks(): jnp.where(valid[:, None, None], incoming, 0.0)  14.3 us
    all_to_all x2, starting transfers between devices, summed_on_arrival(): lax.all_to_all(split_up(array, dim, length), axis, 0, 0, tiled=True)  13.3 us
  transfers between devices with their start and end apart: 13, of which 8 were waited for; matrix products, arithmetic and copies ran while one was open for 41% of the time, Pallas kernels for 0%

commit v1 on v0

v1 whole, which is shorter than its diff:
```python
import functools

import jax
import jax.numpy as jnp
from jax import lax
from jax.experimental import pallas as pl
from jax.experimental.pallas import tpu as pltpu
from jax.sharding import PartitionSpec as P

MESH = pl.DeviceIdType.MESH
CAP = 2
SCALE = 1.0 / 0.07
EPS = 1e-06
ROOT_HALF = 0.7071067811865476
INV_ROOT_TWO_PI = 0.3989422804014327
F32 = jnp.float32
BF16 = jnp.bfloat16
NG, ND = 8, 16
NPEER = NG + ND
SEMS = 320


def split(value):
    hi = value.astype(BF16)
    return hi, (value - hi.astype(F32)).astype(BF16)


def dot(a, b, ca=1, cb=0):
    return lax.dot_general(a, b, (((ca,), (cb,)), ((), ())), preferred_element_type=F32)


def dot3(a, b, ca=1, cb=0):
    return dot(a[0], b[0], ca, cb) + (dot(a[0], b[1], ca, cb) + dot(a[1], b[0], ca, cb))


def prep_kernel(list_ref, sel_ref, tiles_ref, rows_ref, local_ref, acc, onehot, count, meta):
    g, d = lax.axis_index("grp"), lax.axis_index("dev")
    device = g * ND + d
    n_tiles, block = tiles_ref.shape[0], tiles_ref.shape[1]
    sel_dev = sel_ref.shape[0]
    nb = local_ref.shape[2] // block
    rows_ref[...] = jnp.zeros_like(rows_ref)
    acc[...] = jnp.zeros_like(acc)
    lane = lax.broadcasted_iota(jnp.int32, (sel_dev, block), 1)
    sel = sel_ref[...]
    for b in range(nb):
        onehot[b] = (sel == lane + b * block).astype(F32).astype(BF16)
    for p in range(NPEER + 1):
        count[p] = 0
        meta[p] = 0
    for t in range(n_tiles):
        row_block = list_ref[2 * t] - device * nb
        col = list_ref[2 * t + 1]
        owner = col // nb
        col_block = col - owner * nb
        og = owner // ND
        od = owner - og * ND
        local = owner == device
        peer = jnp.where(local, NPEER, jnp.where(og == g, od, ND + og))
        rank = jnp.minimum(count[peer], 1)
        count[peer] = rank + 1
        meta[peer] = meta[peer] + col_block * jnp.where(rank == 0, 1, nb)
        picked = dot(onehot[row_block], tiles_ref[t])
        rows_ref[rank, peer] = picked.astype(BF16)
        acc[col_block] += picked * local.astype(F32)
    for p in range(NPEER):
        rows_ref[2, p] = jnp.full((sel_dev, block), meta[p].astype(F32), F32).astype(BF16)
    for b in range(nb):
        hi, lo = split(acc[b])
        local_ref[0, :, b * block : (b + 1) * block] = hi
        local_ref[1, :, b * block : (b + 1) * block] = lo


class Links:
    def __init__(self, send_sem, recv_sem):
        self.g, self.d = lax.axis_index("grp"), lax.axis_index("dev")
        self.x, self.c = self.g // 2, self.g % 2
        self.y, self.z = self.d // 4, self.d % 4
        self.send_sem, self.recv_sem = send_sem, recv_sem
        self.used, self.copies = 0, []

    def to(self, src, dst, grp=None, dev=None):
        k = self.used
        self.used += 1
        copy = pltpu.make_async_remote_copy(
            src_ref=src,
            dst_ref=dst,
            send_sem=self.send_sem.at[k],
            recv_sem=self.recv_sem.at[k],
            device_id=(self.g if grp is None else grp, self.d if dev is None else dev),
            device_id_type=MESH,
        )
        copy.start()
        self.copies.append(copy)
        return copy

    def pos(self, axis):
        return {"x": self.x, "y": self.y, "z": self.z}[axis]

    def shift(self, src, dst, axis, step):
        if axis == "x":
            return self.to(src, dst, grp=(self.x + step) % 4 * 2 + self.c)
        if axis == "y":
            return self.to(src, dst, dev=(self.y + step) % 4 * 4 + self.z)
        return self.to(src, dst, dev=self.y * 4 + (self.z + step) % 4)

    def core(self, src, dst):
        return self.to(src, dst, grp=self.x * 2 + 1 - self.c)

    def all_dev(self, src, dst):
        out = []
        for i in range(1, ND):
            e = (self.d + i) % ND
            out.append(self.to(src(e), dst, dev=e))
        return out

    def all_grp(self, src, dst):
        out = []
        for i in range(1, NG):
            e = (self.g + i) % NG
            out.append(self.to(src(e), dst, grp=e))
        return out


def arrived(copies):
    for copy in copies:
        copy.wait_recv()


class Ring:
    def __init__(self, links, axis, chunk):
        self.links, self.axis, self.chunk = links, axis, chunk
        r = links.pos(axis)
        self.r, self.up, self.down, self.far = r, (r + 1) % 4, (r + 3) % 4, (r + 2) % 4

    def gather_1(self):
        own = self.chunk(self.r, None)
        self.a = self.links.shift(own, own, self.axis, 1)
        self.b = self.links.shift(own, own, self.axis, 3)

    def gather_2(self):
        self.a.wait_recv()
        part = self.chunk(self.down, 0)
        self.a = self.links.shift(part, part, self.axis, 1)
        self.b.wait_recv()
        part = self.chunk(self.up, 1)
        self.b = self.links.shift(part, part, self.axis, 3)

    def gather_3(self):
        self.a.wait_recv()
        self.b.wait_recv()

    def reduce_1(self, land):
        self.land = land
        send = self.links.shift
        self.a = send(self.chunk(self.far, 0), land(0, 0, 0), self.axis, 1)
        self.b = send(self.chunk(self.far, 1), land(0, 1, 1), self.axis, 3)
        self.a1 = send(self.chunk(self.up, 1), land(1, 0, 1), self.axis, 1)
        self.b1 = send(self.chunk(self.down, 0), land(1, 1, 0), self.axis, 3)

    def reduce_2(self):
        send, land = self.links.shift, self.land
        self.a.wait_recv()
        view = self.chunk(self.up, 0)
        view[...] += land(0, 0, 0)[...]
        self.a = send(view, land(1, 0, 0), self.axis, 1)
        self.b.wait_recv()
        view = self.chunk(self.down, 1)
        view[...] += land(0, 1, 1)[...]
        self.b = send(view, land(1, 1, 1), self.axis, 3)

    def reduce_3(self):
        arrived([self.a, self.b, self.a1, self.b1])
        for s in (0, 1):
            view = self.chunk(self.r, s)
            view[...] += self.land(1, 0, s)[...] + self.land(1, 1, s)[...]


def rows_of(ref, s, cut):
    if s is None:
        return ref
    n = ref.shape[0]
    return ref.at[pl.ds(0, cut)] if s == 0 else ref.at[pl.ds(cut, n - cut)]


class Plane:
    def __init__(self, links, buf):
        y, z = links.y, links.z
        cut = 16
        self.links, self.buf = links, buf

        def big(h):
            def view(i, s):
                some = slice(None) if s is None else pl.ds(2 * s, 2)
                return buf.at[0, i, some] if h == 0 else buf.at[1, some, i]

            return view

        def small(h):
            def view(i, s):
                return rows_of(buf.at[0, y, i] if h == 0 else buf.at[1, i, z], s, cut)

            return view

        self.cut = cut
        self.outer = [Ring(links, "y", big(0)), Ring(links, "z", big(1))]
        self.inner = [Ring(links, "z", small(0)), Ring(links, "y", small(1))]

    def gather(self):
        for name in ("gather_1", "gather_2", "gather_3"):
            for ring in self.inner:
                getattr(ring, name)()
            yield
        for name in ("gather_1", "gather_2", "gather_3"):
            for ring in self.outer:
                getattr(ring, name)()
            yield

    def reduce(self, big, small):
        rows = self.buf.shape[3]
        cut = self.cut

        def land_big(h):
            def view(k, way, s):
                return big.at[h, way, pl.ds(0, 2) if k == 0 else pl.ds(2 + 2 * s, 2)]

            return view

        def land_small(h):
            def view(k, way, s):
                n = (cut, rows - cut)[s]
                start = 0 if k == 0 else (cut if s == 0 else 2 * cut)
                return small.at[h, way, pl.ds(start, n)]

            return view

        for h, ring in enumerate(self.outer):
            ring.reduce_1(land_big(h))
        yield
        for ring in self.outer:
            ring.reduce_2()
        yield
        for h in (0, 1):
            self.outer[h].reduce_3()
            self.inner[h].reduce_1(land_small(h))
        yield
        for ring in self.inner:
            ring.reduce_2()
        yield
        for ring in self.inner:
            ring.reduce_3()
        yield


class Line:
    def __init__(self, links, buf):
        c = links.c
        self.links, self.buf = links, buf
        self.ring = Ring(links, "x", lambda i, s: rows_of(buf.at[i, c], s, 16))

    def gather(self):
        for name in ("gather_1", "gather_2", "gather_3"):
            getattr(self.ring, name)()
            yield
        view = self.buf.at[:, self.links.c]
        copy = self.links.core(view, view)
        yield
        copy.wait_recv()
        yield

    def reduce(self, pair, small):
        rows = self.buf.shape[2]

        def land(k, way, s):
            n = (16, rows - 16)[s]
            return small.at[way, pl.ds(0 if k == 0 else (16 if s == 0 else 32), n)]

        copy = self.links.core(self.buf.at[:, 1 - self.links.c], pair)
        yield
        copy.wait_recv()
        view = self.buf.at[:, self.links.c]
        view[...] += pair[...]
        self.ring.reduce_1(land)
        yield
        self.ring.reduce_2()
        yield
        self.ring.reduce_3()
        yield


def together(*runs):
    runs = list(runs)
    while runs:
        runs = [run for run in runs if next(run, "end") != "end"]


def main_kernel(
    rows_ref, local_ref, nodes_ref, weight_ref, texts_ref, sel_ref, sel_list, pair_ref,
    loss_ref, gn_ref, gw_ref, gt_ref,
    near_in, far_in, spread, spread_t, rounded, wh, wl,
    npart, nbig, nsmall, fpart, fpair, fsmall,
    units, cols, pairs, spart, sbig, ssmall, tpart, tpair, tsmall,
    row_in, col_in, loss_dev, loss_grp, g_near, g_far,
    gpart, gpair, gbig, gsmall, gx, gfull, chosen,
    send_sem, recv_sem,
):
    links = Links(send_sem, recv_sem)
    g, d, x, c, y, z = links.g, links.d, links.x, links.c, links.y, links.z
    sel_dev, feat = texts_ref.shape
    half = feat // 2
    nodes_dev = nodes_ref.shape[0]
    block = near_in.shape[3]
    nb = nodes_dev // block
    total_sel = sel_dev * NG * ND

    barrier = pltpu.get_barrier_semaphore()
    for i in range(1, ND):
        pl.semaphore_signal(barrier, inc=1, device_id=(g, (d + i) % ND), device_id_type=MESH)
    for i in range(1, NG):
        pl.semaphore_signal(barrier, inc=1, device_id=((g + i) % NG, d), device_id_type=MESH)

    texts = texts_ref[...]
    text_norm = jnp.sqrt(jnp.sum(texts * texts, axis=1, keepdims=True) + EPS)
    unit_texts = texts / text_norm
    cols[x, c] = unit_texts
    pairs[d] = jnp.broadcast_to(pair_ref[...], (sel_dev, block))
    near_in[:, d] = jnp.zeros((3, sel_dev, block), BF16)
    far_in[:, g] = jnp.zeros((3, sel_dev, block), BF16)
    pl.semaphore_wait(barrier, ND + NG - 2)

    near_copies = links.all_dev(lambda e: rows_ref.at[:, e], near_in.at[:, d])
    far_copies = links.all_grp(lambda e: rows_ref.at[:, ND + e], far_in.at[:, g])
    text_run = Line(links, cols).gather()
    next(text_run)
    pair_copies = links.all_dev(lambda e: pairs.at[d], pairs.at[d])

    rounded[...] = nodes_ref[...].astype(BF16)
    whole = weight_ref[...]
    hi, lo = split(whole)
    wh[...] = hi
    wl[...] = lo
    for k in range(sel_dev):
        chosen[pl.ds(k, 1), :] = nodes_ref[pl.ds(sel_list[k], 1), :]
    next(text_run)

    def expand(into, rows):
        tag = rows[2].astype(F32)
        second = jnp.floor(tag * (1.0 / nb) + 0.01)
        first = tag - second * nb
        for q, which in ((0, first), (1, second)):
            for b in range(nb):
                spread[q, into, :, b * block : (b + 1) * block] = jnp.where(
                    which == float(b), rows[q].astype(F32), 0.0
                ).astype(BF16)

    arrived(near_copies)
    for p in range(ND):
        expand(p, near_in[:, p])
    spread[0, d] = local_ref[0]
    spread[1, d] = local_ref[1]
    flat = (ND * sel_dev, nb * block)
    s0, s1 = spread[0, :ND].reshape(flat), spread[1, :ND].reshape(flat)
    for h in (0, 1):
        table = rounded[:, h * half : (h + 1) * half]
        npart[h] = (dot(s0, table) + dot(s1, table)).reshape(4, 4, sel_dev, half)
    near_run = Plane(links, npart).reduce(nbig, nsmall)
    next(near_run)
    arrived(far_copies)
    for p in range(NG):
        expand(ND + p, far_in[:, p])
    flat = (NG * sel_dev, nb * block)
    s0, s1 = spread[0, ND:].reshape(flat), spread[1, ND:].reshape(flat)
    fpart[...] = (dot(s0, rounded[...]) + dot(s1, rounded[...])).reshape(4, 2, sel_dev, feat)
    far_run = Line(links, fpart).reduce(fpair, fsmall)
    next(far_run)
    some = 128 // sel_dev
    for q in (0, 1):
        for i in range(NPEER // some):
            rows = spread[q, i * some : (i + 1) * some].reshape(128, nb * block)
            spread_t[q, :, i * 128 : (i + 1) * 128] = rows.astype(F32).T.astype(BF16)
    together(near_run, far_run, text_run)

    far_sum = fpart[x, c]
    for h in (0, 1):
        take = slice(h * half, (h + 1) * half)
        own = npart[h, y, z]
        chosen[:, take] += own + far_sum[:, take]
    picked = chosen[...]
    picked_parts = split(picked)
    before = dot3(picked_parts, (wh[...], wl[...]))
    curve = 0.5 * (1.0 + lax.erf(before * ROOT_HALF))
    hidden = before * curve
    node_norm = jnp.sqrt(jnp.sum(hidden * hidden, axis=1, keepdims=True) + EPS)
    unit_nodes = hidden / node_norm
    for h in (0, 1):
        units[h, y, z] = unit_nodes[:, h * half : (h + 1) * half]
    unit_run = Plane(links, units).gather()
    next(unit_run)
    arrived(pair_copies)
    col_parts = split(cols[...].reshape(NG * sel_dev, feat))
    together(unit_run)

    rows_all = ND * sel_dev
    cols_all = NG * sel_dev
    unit_parts = [split(units[h].reshape(rows_all, half)) for h in (0, 1)]
    scores = 0.0
    for h in (0, 1):
        text_half = tuple(v[:, h * half : (h + 1) * half] for v in col_parts)
        scores += dot3(unit_parts[h], text_half, 1, 1)
    scores = SCALE * scores
    exps = jnp.exp(scores)
    row_sum = jnp.sum(exps, axis=1, keepdims=True)
    row_in[d] = jnp.broadcast_to(row_sum, (rows_all, 128)).T[:8]
    row_copies = links.all_dev(lambda e: row_in.at[d], row_in.at[d])
    col_in[g] = jnp.broadcast_to(jnp.sum(exps, axis=0, keepdims=True), (8, cols_all))
    col_copies = links.all_grp(lambda e: col_in.at[g], col_in.at[g])
    lane = lax.broadcasted_iota(jnp.int32, (sel_dev, cols_all), 1)
    ids = (lane // sel_dev * ND + d) * sel_dev + lane % sel_dev
    target = (pairs[...].reshape(rows_all, block)[:, :1] == ids[:1]).astype(F32)
    positive = jnp.sum(jnp.sum(target * scores, axis=1, keepdims=True), axis=0, keepdims=True)
    arrived(col_copies)
    col_total = jnp.sum(col_in[...], axis=0)
    arrived(row_copies)
    row_total = jnp.sum(row_in[...], axis=0)
    log_rows = jnp.sum(jnp.log(row_total[:1]), axis=1, keepdims=True)
    log_cols = jnp.sum(jnp.log(col_total[:1]), axis=1, keepdims=True)
    part = (log_rows / ND + log_cols / NG) / (2.0 * total_sel) - positive / total_sel
    loss_dev[d] = jnp.broadcast_to(part, (8, 128))
    row_recip = jnp.broadcast_to(1.0 / row_total[:1], (128, rows_all)).T[:, :1]
    col_recip = 1.0 / col_total[:1]
    slope = 0.5 * exps * (row_recip + col_recip) - target
    slope_parts = split(slope)
    for h in (0, 1):
        text_half = tuple(v[:, h * half : (h + 1) * half] for v in col_parts)
        spart[h] = dot3(slope_parts, text_half).reshape(4, 4, sel_dev, half)
    node_run = Plane(links, spart).reduce(sbig, ssmall)
    next(node_run)
    for h in (0, 1):
        grown = dot3(slope_parts, unit_parts[h], 0, 0)
        tpart[:, :, :, h * half : (h + 1) * half] = grown.reshape(4, 2, sel_dev, half)
    loss_copies = links.all_dev(lambda e: loss_dev.at[d], loss_dev.at[d])
    together(node_run, Line(links, tpart).reduce(tpair, tsmall))
    arrived(loss_copies)
    loss_grp[g] = jnp.sum(loss_dev[...], axis=0)
    loss_copies = links.all_grp(lambda e: loss_grp.at[g], loss_grp.at[g])

    node_dir = SCALE * jnp.concatenate([spart[0, y, z], spart[1, y, z]], axis=1)
    node_back = (
        node_dir - unit_nodes * jnp.sum(unit_nodes * node_dir, axis=1, keepdims=True)
    ) / node_norm
    pre_grad = node_back * (curve + before * jnp.exp(-0.5 * before * before) * INV_ROOT_TWO_PI)
    pre_parts = split(pre_grad)
    row_grads = dot3(pre_parts, (wh[...], wl[...]), 1, 1)
    grads = row_grads.astype(BF16)
    for h in (0, 1):
        g_near[h, y, z] = grads[:, h * half : (h + 1) * half]
    g_far[x, c] = grads
    near_run = Plane(links, g_near).gather()
    far_run = Line(links, g_far).gather()
    next(near_run)
    next(far_run)

    deep = 2 * 16
    piece = feat // deep
    for h in (0, 1):
        right = tuple(v[:, h * half : (h + 1) * half] for v in pre_parts)
        gpart[:, h] = dot3(picked_parts, right, 0, 0).reshape(2, 4, 4, piece, half)
    copy = links.core(gpart.at[1 - c], gpair)
    next(near_run)
    next(far_run)
    copy.wait_recv()
    mine = gpart.at[c]
    mine[...] += gpair[...]
    plane = Plane(links, mine)
    weight_run = plane.reduce(gbig, gsmall)
    next(weight_run)
    together(near_run, far_run, weight_run)
    gx[x] = gpart[c, :, y, z]
    copies = []
    for i in (1, 2, 3):
        copies.append(links.shift(gx.at[x], gx.at[x], "x", i))

    text_dir = SCALE * tpart[x, c]
    gt_ref[...] = (
        text_dir - unit_texts * jnp.sum(unit_texts * text_dir, axis=1, keepdims=True)
    ) / text_norm
    arrived(copies)
    gfull[c, :, y, z] = gx[0] + gx[1] + gx[2] + gx[3]
    weight_run = Plane(links, gfull.at[c]).gather()
    next(weight_run)

    spot = lax.broadcasted_iota(jnp.int32, (sel_dev, nodes_dev), 1)
    hot = (sel_ref[...] == spot).astype(F32).astype(BF16)
    top, mid = split(row_grads)
    low = (row_grads - top.astype(F32) - mid.astype(F32)).astype(BF16)
    steps = [lambda: next(weight_run), lambda: next(weight_run)]
    for h in (0, 1):
        take = slice(h * half, (h + 1) * half)
        near = g_near[h].reshape(ND * sel_dev, half)
        far = g_far[:, :, :, take].reshape(NG * sel_dev, half)
        edge = ND * sel_dev
        total = dot(spread_t[0, :, :edge], near) + dot(spread_t[1, :, :edge], near)
        total += dot(spread_t[0, :, edge:], far) + dot(spread_t[1, :, edge:], far)
        total += dot(hot, top[:, take], 0, 0) + dot(hot, mid[:, take], 0, 0)
        gn_ref[:, take] = total + dot(hot, low[:, take], 0, 0)
        steps[h]()
    together(weight_run)
    view = gfull.at[c]
    copy = links.core(view, view)
    arrived(loss_copies)
    loss_ref[...] = jnp.sum(loss_grp[...], axis=0)
    copy.wait_recv()
    rows_half = feat // 2
    for core in (0, 1):
        for h in (0, 1):
            gw_ref[core * rows_half : (core + 1) * rows_half, h * half : (h + 1) * half] = gfull[
                core, h
            ].reshape(rows_half, half)
    for copy in links.copies:
        copy.wait_send()


def shards(node_features, tiles, tile_list, weight, texts, selected, pairing):
    device = lax.axis_index("grp") * ND + lax.axis_index("dev")
    tile_dev, block = tiles.shape[0], tiles.shape[1]
    nodes_dev, feat = node_features.shape
    sel_dev = selected.shape[0]
    nb = nodes_dev // block
    half = feat // 2
    piece = feat // 32
    my_list = lax.dynamic_slice_in_dim(tile_list, device * tile_dev, tile_dev, 0).reshape(-1)
    sel_own = selected - device * nodes_dev
    sel_col = sel_own.reshape(sel_dev, 1)
    vmem = pl.BlockSpec(memory_space=pltpu.VMEM)
    smem = pl.BlockSpec(memory_space=pltpu.SMEM)
    rows, local = pl.pallas_call(
        prep_kernel,
        out_shape=(
            jax.ShapeDtypeStruct((3, NPEER + 1, sel_dev, block), BF16),
            jax.ShapeDtypeStruct((2, sel_dev, nb * block), BF16),
        ),
        in_specs=[smem, vmem, vmem],
        out_specs=(vmem, vmem),
        scratch_shapes=[
            pltpu.VMEM((nb, sel_dev, block), F32),
            pltpu.VMEM((nb, sel_dev, block), BF16),
            pltpu.SMEM((NPEER + 1,), jnp.int32),
            pltpu.SMEM((NPEER + 1,), jnp.int32),
        ],
        compiler_params=pltpu.CompilerParams(vmem_limit_bytes=16 * 2**20),
    )(my_list, sel_col, tiles)

    def f32(*shape):
        return pltpu.VMEM(shape, F32)

    def bf16(*shape):
        return pltpu.VMEM(shape, BF16)

    def plane_buffers(rows):
        return [
            f32(2, 2, 6, rows, half),
            f32(2, 2, 16 + rows, half),
        ]

    def line_buffers():
        return [f32(4, 2, sel_dev, feat), f32(4, sel_dev, feat), f32(2, 16 + sel_dev, feat)]

    loss, grad_nodes, grad_weight, grad_texts = pl.pallas_call(
        main_kernel,
        out_shape=(
            jax.ShapeDtypeStruct((8, 128), F32),
            jax.ShapeDtypeStruct((nodes_dev, feat), F32),
            jax.ShapeDtypeStruct((feat, feat), F32),
            jax.ShapeDtypeStruct((sel_dev, feat), F32),
        ),
        in_specs=[vmem] * 6 + [smem, vmem],
        out_specs=(vmem,) * 4,
        scratch_shapes=[
            bf16(3, ND, sel_dev, block),
            bf16(3, NG, sel_dev, block),
            bf16(2, NPEER, sel_dev, nb * block),
            bf16(2, nb * block, NPEER * sel_dev),
            bf16(nodes_dev, feat),
            bf16(feat, feat),
            bf16(feat, feat),
            f32(2, 4, 4, sel_dev, half),
            *plane_buffers(sel_dev),
            *line_buffers(),
            f32(2, 4, 4, sel_dev, half),
            f32(4, 2, sel_dev, feat),
            pltpu.VMEM((ND, sel_dev, block), jnp.int32),
            f32(2, 4, 4, sel_dev, half),
            *plane_buffers(sel_dev),
            *line_buffers(),
            f32(ND, 8, ND * sel_dev),
            f32(NG, 8, NG * sel_dev),
            f32(ND, 8, 128),
            f32(NG, 8, 128),
            bf16(2, 4, 4, sel_dev, half),
            bf16(4, 2, sel_dev, feat),
            f32(2, 2, 4, 4, piece, half),
            f32(2, 4, 4, piece, half),
            *plane_buffers(piece),
            f32(4, 2, piece, half),
            f32(2, 2, 4, 4, piece, half),
            f32(sel_dev, feat),
            pltpu.SemaphoreType.DMA((SEMS,)),
            pltpu.SemaphoreType.DMA((SEMS,)),
        ],
        compiler_params=pltpu.CompilerParams(
            collective_id=0, has_side_effects=True, vmem_limit_bytes=60 * 2**20
        ),
    )(rows, local, node_features, weight, texts, sel_col, sel_own, pairing.reshape(sel_dev, 1))
    return loss[0, 0], grad_nodes, grad_weight, grad_texts


def solution(mesh):
    both = ("grp", "dev")
    placed = (
        P(both, None),
        P(both, None, None),
        P(),
        P(),
        P(both, None),
        P(both),
        P(both),
    )
    return jax.shard_map(
        shards,
        mesh=mesh,
        in_specs=placed,
        out_specs=(P(), P(both, None), P(), P(both, None)),
        check_vma=False,
    )
```

time: 438 us -> 152 us (0.35)
  Pallas kernels: 0 us -> 138 us
  other arithmetic: 123 us -> 1.82 us
  waiting for transfers between devices: 90.7 us -> 0 us
  starting transfers between devices: 74.5 us -> 0 us
  matrix products: 50.8 us -> 0 us
  blocking collectives: 44.3 us -> 0 us
  local copies, waits for them, and re-layouts: 34.1 us -> 11.5 us
  between operations: 18.3 us -> 0.7 us
    pallas_call x0 -> x2, Pallas kernels: none -> 138 us  [the longest x1 136 us: shards(): pl.pallas_call(main_kernel, out_shape=(jax.ShapeDtypeStruct((8, 128), F32...]
    scatter-add x4 -> x0, other arithmetic: 93.4 us -> none  [the longest x1 46.8 us: shards(): grad_blocks = empty_blocks.at[col_block].add(local_spread)]
    all_to_all x12 -> x0, starting transfers between devices: 74.5 us -> none  [the longest x6 37.2 us: from_everyone(): return lax.all_to_all(copies, axis, split_axis=0, concat_axis=0, tiled=True)]
    all_to_all x12 -> x0, waiting for transfers between devices: 68.7 us -> none  [the longest x6 38.2 us: from_everyone(): return lax.all_to_all(copies, axis, split_axis=0, concat_axis=0, tiled=True)]
    dot_general x14 -> x0, matrix products: 50.8 us -> none  [the longest x1 8.71 us: shards(): jnp.einsum('tkc,kd->tcd', local_tile_rows, rounded_grads, preferred_eleme...]
    psum x6 -> x0, blocking collectives: 44.3 us -> none  [over_axes(): return functools.reduce(lax.psum, axes, array)]
    psum x1 -> x0, waiting for transfers between devices: 22 us -> none  [shards(): grad_weight = lax.psum(weight_term, GRP_DEV)]
    gather x5 -> x0, local copies, waits for them, and re-layouts: 17.5 us -> none  [the longest x1 6.57 us: shards(): local_sources = jnp.take(rounded, col_block, axis=0)]
  transfers between devices with their start and end apart: 13 -> 0, of which waited for: 8 -> 0; matrix products, arithmetic and copies ran while one was open for 41% -> 0% of each run, Pallas kernels for 0% -> 0%
where the time goes in v1:
time: 152 us
  Pallas kernels  138 us (91%)
  local copies, waits for them, and re-layouts  11.5 us (8%)
  other arithmetic  1.82 us (1%)
    pallas_call x1, Pallas kernels, shards(): pl.pallas_call(main_kernel, out_shape=(jax.ShapeDtypeStruct((8, 128), F32...  136 us
    unnamed x17, local copies, waits for them, and re-layouts  8.41 us

profile of v1, /device:TPU:1, one launch (start us, length us, event | category | flops | bytes accessed | tf_op | source)
XLA Modules:
  0.0 152.0 jit_solution(1079621784890904986)
XLA Ops:
  0.6 0.0 copy-start
  0.7 0.8 copy-done
  1.4 0.1 constant_dynamic-slice_fusion
  1.5 0.7 fusion
  2.2 1.2 broadcast_subtract_fusion.sel_list
  3.3 0.1 copy.16.sel_ref
  3.4 0.0 copy-start.3
  3.4 1.3 copy.18.pair_ref
  4.8 0.1 copy.15
  4.9 0.1 reshape.17.list_ref
  5.0 0.0 copy-start.1
  5.0 1.4 copy-done.1
  6.5 1.7 %shard_map.102 = (bf16[3,25,32,128]{3,2,1,0:T(8,128)(2,1)S(1)}, bf16[2,32,512]{2,1,0:T(8,128)(2,1)S(1)}) custom-call(s32[104]{0:T(128)S(1)} %reshape.17.list_ref, s32[32,1]{1,0:T(8,128)S(1)} %copy.16.sel_ref, bf16[52,128,128]{2,1,0:T(8,128)(2,1)S(1)} %copy-done.1), custom_call_target="tpu_custom_call" | custom-call | tf_op jit(solution)/shard_map/pallas_call | solution.py:536
  8.1 0.0 copy-start.2
  8.1 0.8 copy-done.2
  9.0 0.0 copy-start.4
  9.0 0.6 copy-done.4
  9.6 0.0 copy-done.3
  9.6 136.3 %shard_map.103 = (f32[8,128]{1,0:T(8,128)}, f32[512,768]{1,0:T(8,128)}, f32[768,768]{1,0:T(8,128)}, f32[32,768]{1,0:T(8,128)}) custom-call(bf16[3,25,32,128]{3,2,1,0:T(8,128)(2,1)} %copy-done.2, bf16[2,32,512]{2,1,0:T(8,128)(2,1)} %copy-done.4, f32[512,768]{1,0:T(8,128)} %nodes_ref.1, f32[768,768]{1,0:T(8,128)} %weight_ref.1, f32[32,768]{1,0:T(8,128)} %texts_ref.1, ...), custom_call_target="tpu_custom_call" | custom-call | tf_op jit(solution)/shard_map/pallas_call | solution.py:568
  145.9 0.0 copy-start.5
  145.9 1.3 slice.3
  147.3 2.7 %copy.22 = f32[512,768]{1,0:T(8,128)} copy(f32[512,768]{1,0:T(8,128)} %get-tuple-element.21) | data formatting | bytes 3145728
  149.9 0.0 copy-done.5
  149.9 0.0 copy-start.6
  149.9 1.4 copy.23
  151.3 0.0 copy-done.6
  151.3 0.6 copy.24
Async XLA Ops:
  0.6 0.8 copy-start
  3.4 6.2 %copy-start.3 = (s32[32,1]{1,0:T(8,128)}, s32[32,1]{1,0:T(8,128)S(1)}, u32[]{:S(2)}) copy-start(s32[32,1]{1,0:T(8,128)S(1)} %copy.16.sel_ref) | copy-start | bytes 388
  5.0 1.5 copy-start.1
  8.1 0.8 copy-start.2
  9.0 0.6 copy-start.4
  145.9 4.0 %copy-start.5 = (f32[768,768]{1,0:T(8,128)S(1)}, f32[768,768]{1,0:T(8,128)}, u32[]{:S(2)}) copy-start(f32[768,768]{1,0:T(8,128)} %get-tuple-element.22) | copy-start | bytes 7077892
  149.9 1.4 copy-start.6

commit v2 on v1

v2 whole, which is shorter than its diff:
```python
import functools

import jax
import jax.numpy as jnp
from jax import lax
from jax.experimental import pallas as pl
from jax.experimental.pallas import tpu as pltpu
from jax.sharding import PartitionSpec as P

MESH = pl.DeviceIdType.MESH
CAP = 2
SCALE = 1.0 / 0.07
EPS = 1e-06
ROOT_HALF = 0.7071067811865476
INV_ROOT_TWO_PI = 0.3989422804014327
F32 = jnp.float32
BF16 = jnp.bfloat16
NG, ND = 8, 16
NPEER = NG + ND
SEMS = 384


def split(value):
    hi = value.astype(BF16)
    return hi, (value - hi.astype(F32)).astype(BF16)


def dot(a, b, ca=1, cb=0):
    return lax.dot_general(a, b, (((ca,), (cb,)), ((), ())), preferred_element_type=F32)


def dot3(a, b, ca=1, cb=0):
    return dot(a[0], b[0], ca, cb) + (dot(a[0], b[1], ca, cb) + dot(a[1], b[0], ca, cb))


def prep_kernel(
    list_ref, sel_ref, pair_ref, tiles_ref, nodes_ref,
    rows_ref, local_ref, rounded_ref, chosen_ref, spot_ref,
    acc, onehot, column, count, meta,
):
    g, d = lax.axis_index("grp"), lax.axis_index("dev")
    device = g * ND + d
    n_tiles, block = tiles_ref.shape[0], tiles_ref.shape[1]
    sel_dev = sel_ref.shape[0]
    nodes_dev = nodes_ref.shape[0]
    nb = nodes_dev // block
    rows_ref[...] = jnp.zeros_like(rows_ref)
    acc[...] = jnp.zeros_like(acc)
    for k in range(sel_dev):
        own = sel_ref[k] - device * nodes_dev
        spot_ref[pl.ds(k, 1), :] = jnp.full((1, block), own, jnp.int32)
        column[pl.ds(k, 1), :] = jnp.full((1, block), pair_ref[k], jnp.int32)
        chosen_ref[pl.ds(k, 1), :] = nodes_ref[pl.ds(own, 1), :]
    lane = lax.broadcasted_iota(jnp.int32, (sel_dev, block), 1)
    sel = spot_ref[...]
    for b in range(nb):
        onehot[b] = (sel == lane + b * block).astype(F32).astype(BF16)
    for p in range(NPEER + 1):
        count[p] = 0
        meta[p] = 0
    for t in range(n_tiles):
        row_block = list_ref[2 * t] - device * nb
        col = list_ref[2 * t + 1]
        owner = col // nb
        col_block = col - owner * nb
        og = owner // ND
        od = owner - og * ND
        local = owner == device
        peer = jnp.where(local, NPEER, jnp.where(og == g, od, ND + og))
        rank = jnp.minimum(count[peer], 1)
        count[peer] = rank + 1
        meta[peer] = meta[peer] + col_block * jnp.where(rank == 0, 1, nb)
        picked = dot(onehot[row_block], tiles_ref[t])
        rows_ref[rank, peer] = picked.astype(BF16)
        acc[col_block] += picked * local.astype(F32)
    pair = column[...]
    high = pair // 64
    tag = jnp.where(lane == 1, high, pair - high * 64)
    for p in range(NPEER):
        rows_ref[2, p] = jnp.where(lane == 0, meta[p], tag).astype(F32).astype(BF16)
    rows_ref[2, d] = jnp.where(lane == 0, 0, tag).astype(F32).astype(BF16)
    for b in range(nb):
        hi, lo = split(acc[b])
        local_ref[0, :, b * block : (b + 1) * block] = hi
        local_ref[1, :, b * block : (b + 1) * block] = lo
    rounded_ref[...] = nodes_ref[...].astype(BF16)


class Links:
    def __init__(self, send_sem, recv_sem):
        self.g, self.d = lax.axis_index("grp"), lax.axis_index("dev")
        self.x, self.c = self.g // 2, self.g % 2
        self.y, self.z = self.d // 4, self.d % 4
        self.send_sem, self.recv_sem = send_sem, recv_sem
        self.used, self.copies = 0, []

    def to(self, src, dst, grp=None, dev=None):
        k = self.used
        self.used += 1
        copy = pltpu.make_async_remote_copy(
            src_ref=src,
            dst_ref=dst,
            send_sem=self.send_sem.at[k],
            recv_sem=self.recv_sem.at[k],
            device_id=(self.g if grp is None else grp, self.d if dev is None else dev),
            device_id_type=MESH,
        )
        copy.start()
        self.copies.append(copy)
        return copy

    def pos(self, axis):
        return {"x": self.x, "y": self.y, "z": self.z}[axis]

    def shift(self, src, dst, axis, step):
        if axis == "x":
            return self.to(src, dst, grp=(self.x + step) % 4 * 2 + self.c)
        if axis == "y":
            return self.to(src, dst, dev=(self.y + step) % 4 * 4 + self.z)
        return self.to(src, dst, dev=self.y * 4 + (self.z + step) % 4)

    def core(self, src, dst):
        return self.to(src, dst, grp=self.x * 2 + 1 - self.c)

    def all_dev(self, src, dst):
        out = []
        for i in range(1, ND):
            e = (self.d + i) % ND
            out.append(self.to(src(e), dst, dev=e))
        return out

    def all_grp(self, src, dst):
        out = []
        for i in range(1, NG):
            e = (self.g + i) % NG
            out.append(self.to(src(e), dst, grp=e))
        return out


def arrived(copies):
    for copy in copies:
        copy.wait_recv()


class Ring:
    def __init__(self, links, axis, chunk):
        self.links, self.axis, self.chunk = links, axis, chunk
        r = links.pos(axis)
        self.r, self.up, self.down, self.far = r, (r + 1) % 4, (r + 3) % 4, (r + 2) % 4

    def gather_1(self):
        own = self.chunk(self.r, None)
        self.a = self.links.shift(own, own, self.axis, 1)
        self.b = self.links.shift(own, own, self.axis, 3)

    def gather_2(self):
        self.a.wait_recv()
        part = self.chunk(self.down, 0)
        self.a = self.links.shift(part, part, self.axis, 1)
        self.b.wait_recv()
        part = self.chunk(self.up, 1)
        self.b = self.links.shift(part, part, self.axis, 3)

    def gather_3(self):
        self.a.wait_recv()
        self.b.wait_recv()

    def reduce_1(self, land):
        self.land = land
        send = self.links.shift
        self.a = send(self.chunk(self.far, 0), land(0, 0, 0), self.axis, 1)
        self.b = send(self.chunk(self.far, 1), land(0, 1, 1), self.axis, 3)
        self.a1 = send(self.chunk(self.up, 1), land(1, 0, 1), self.axis, 1)
        self.b1 = send(self.chunk(self.down, 0), land(1, 1, 0), self.axis, 3)

    def reduce_2(self):
        send, land = self.links.shift, self.land
        self.a.wait_recv()
        view = self.chunk(self.up, 0)
        view[...] += land(0, 0, 0)[...]
        self.a = send(view, land(1, 0, 0), self.axis, 1)
        self.b.wait_recv()
        view = self.chunk(self.down, 1)
        view[...] += land(0, 1, 1)[...]
        self.b = send(view, land(1, 1, 1), self.axis, 3)

    def reduce_3(self):
        arrived([self.a, self.b, self.a1, self.b1])
        for s in (0, 1):
            view = self.chunk(self.r, s)
            view[...] += self.land(1, 0, s)[...] + self.land(1, 1, s)[...]


def rows_of(ref, s, cut):
    if s is None:
        return ref
    n = ref.shape[0]
    return ref.at[pl.ds(0, cut)] if s == 0 else ref.at[pl.ds(cut, n - cut)]


class Plane:
    def __init__(self, links, buf):
        self.links, self.buf = links, buf
        self.outer, self.inner = ("y", "z"), ("z", "y")

    def at(self, h, out, into):
        links = self.links
        out = (links.pos(self.outer[h]) + out) % 4
        into = (links.pos(self.inner[h]) + into) % 4
        return self.buf.at[0, out, into] if h == 0 else self.buf.at[1, into, out]

    def gather(self, relay=lambda view: None):
        shift, at, outer, inner = self.links.shift, self.at, self.outer, self.inner
        halves = (0, 1)
        first, far, out, onward = {}, {}, {}, {}

        def send_out(h, o):
            view = at(h, 0, o)
            out[h, o] = shift(view, view, outer[h], 1), shift(view, view, outer[h], 3)
            relay(view)

        def landed(h, o):
            for k, side in ((0, 3), (1, 1)):
                out[h, o][k].wait_recv()
                view = at(h, side, o)
                if (o in (0, 3)) == (side == 3):
                    onward[h, o] = shift(view, view, outer[h], 1 if side == 3 else 3)
                relay(view)

        for h in halves:
            view = at(h, 0, 0)
            first[h] = shift(view, view, inner[h], 1), shift(view, view, inner[h], 3)
        for h in halves:
            send_out(h, 0)
        yield
        for h in halves:
            first[h][0].wait_recv()
            view = at(h, 0, 3)
            far[h] = shift(view, view, inner[h], 1)
            send_out(h, 3)
            first[h][1].wait_recv()
            send_out(h, 1)
        yield
        for h in halves:
            landed(h, 0)
        for h in halves:
            far[h].wait_recv()
            send_out(h, 2)
        yield
        for o in (3, 1):
            for h in halves:
                landed(h, o)
        yield
        for h in halves:
            landed(h, 2)
        yield
        for o in (0, 3, 1, 2):
            for h in halves:
                onward[h, o].wait_recv()
                relay(at(h, 2, o))
        yield

    def reduce(self, land):
        shift, at, outer, inner = self.links.shift, self.at, self.outer, self.inner
        order = (2, 3, 1, 0)
        early, direct, late, last = {}, {}, {}, {}

        def way(o):
            return 1 if o in (2, 3) else 3

        for o in order:
            for h in (0, 1):
                w = way(o)
                early[h, o] = shift(at(h, 2, o), land.at[h, o], outer[h], w)
                direct[h, o] = shift(at(h, 4 - w, o), land.at[h, 4 + o], outer[h], 4 - w)
        yield
        for o in order:
            for h in (0, 1):
                w = way(o)
                early[h, o].wait_recv()
                view = at(h, w, o)
                view[...] += land[h, o]
                late[h, o] = shift(view, land.at[h, 8 + o], outer[h], w)
            if o == 3:
                yield
        yield
        for o in order:
            for h in (0, 1):
                direct[h, o].wait_recv()
                late[h, o].wait_recv()
                view = at(h, 0, o)
                total = view[...] + land[h, 4 + o] + land[h, 8 + o]
                if o == 1:
                    last[h, 2].wait_recv()
                    total += land[h, 12]
                view[...] = total
                if o == 2:
                    last[h, 2] = shift(view, land.at[h, 12], inner[h], 1)
                if o == 3:
                    last[h, 3] = shift(view, land.at[h, 14], inner[h], 3)
                if o == 1:
                    last[h, 1] = shift(view, land.at[h, 13], inner[h], 1)
            yield
        for h in (0, 1):
            last[h, 1].wait_recv()
            last[h, 3].wait_recv()
            view = at(h, 0, 0)
            view[...] += land[h, 13] + land[h, 14]
        yield


class Line:
    def __init__(self, links, buf):
        c = links.c
        self.links, self.buf = links, buf
        self.ring = Ring(links, "x", lambda i, s: rows_of(buf.at[i, c], s, 16))

    def gather(self):
        for name in ("gather_1", "gather_2", "gather_3"):
            getattr(self.ring, name)()
            yield
        view = self.buf.at[:, self.links.c]
        copy = self.links.core(view, view)
        yield
        copy.wait_recv()
        yield

    def reduce(self, pair, small):
        rows = self.buf.shape[2]

        def land(k, way, s):
            n = (16, rows - 16)[s]
            return small.at[way, pl.ds(0 if k == 0 else (16 if s == 0 else 32), n)]

        copy = self.links.core(self.buf.at[:, 1 - self.links.c], pair)
        yield
        copy.wait_recv()
        view = self.buf.at[:, self.links.c]
        view[...] += pair[...]
        self.ring.reduce_1(land)
        yield
        self.ring.reduce_2()
        yield
        self.ring.reduce_3()
        yield


def together(*runs):
    runs = list(runs)
    while runs:
        runs = [run for run in runs if next(run, "end") != "end"]


def to_lanes(column):
    n = column.shape[0]
    wide = jnp.broadcast_to(column, (n, 128)).T
    rows = [wide[:1, 128 * i : 128 * (i + 1)] for i in range(n // 128)]
    return jnp.concatenate(rows + [jnp.zeros((8 - len(rows), 128), F32)], axis=0)


def as_row(packed, n):
    return jnp.concatenate([packed[i : i + 1] for i in range(n // 128)], axis=1)


def main_kernel(
    rows_ref, local_ref, rounded, chosen0, spot_ref, weight_ref, texts_ref,
    loss_ref, gn_ref, gw_ref, gt_ref,
    near_in, far_in, spread, spread_t, wh, wl,
    npart, nland, fpart, fpair, fsmall,
    units, cols, spart, sland, tpart, tpair, tsmall,
    row_in, col_in, loss_dev, loss_grp, slices_out, slices, pre_all, pre_stack, g_far,
    gpart, gpair, gx, gfull, chosen,
    send_sem, recv_sem,
):
    links = Links(send_sem, recv_sem)
    g, d, x, c, y, z = links.g, links.d, links.x, links.c, links.y, links.z
    sel_dev, feat = texts_ref.shape
    half = feat // 2
    nodes_dev = rounded.shape[0]
    block = near_in.shape[3]
    nb = nodes_dev // block
    total_sel = sel_dev * NG * ND
    rows_all = ND * sel_dev
    cols_all = NG * sel_dev
    takes = [slice(h * half, (h + 1) * half) for h in (0, 1)]

    barrier = pltpu.get_barrier_semaphore()
    for i in range(1, ND):
        pl.semaphore_signal(barrier, inc=1, device_id=(g, (d + i) % ND), device_id_type=MESH)
    for i in range(1, NG):
        pl.semaphore_signal(barrier, inc=1, device_id=((g + i) % NG, d), device_id_type=MESH)

    texts = texts_ref[...]
    text_norm = jnp.sqrt(jnp.sum(texts * texts, axis=1, keepdims=True) + EPS)
    unit_texts = texts / text_norm
    cols[x, c] = unit_texts
    near_in[:2, d] = jnp.zeros((2, sel_dev, block), BF16)
    near_in[2, d] = rows_ref[2, d]
    far_in[:, g] = jnp.zeros((3, sel_dev, block), BF16)
    pl.semaphore_wait(barrier, ND + NG - 2)

    near_copies = links.all_dev(lambda e: rows_ref.at[:, e], near_in.at[:, d])
    far_copies = links.all_grp(lambda e: rows_ref.at[:, ND + e], far_in.at[:, g])
    text_run = Line(links, cols).gather()
    next(text_run)
    hi, lo = split(weight_ref[...])
    wh[...] = hi
    wl[...] = lo

    def expand(into, rows):
        tag = rows[2].astype(F32)[:, :1]
        second = jnp.floor(tag * (1.0 / nb) + 0.01)
        first = tag - second * nb
        for q, which in ((0, first), (1, second)):
            for b in range(nb):
                spread[q, into, :, b * block : (b + 1) * block] = jnp.where(
                    which == float(b), rows[q].astype(F32), 0.0
                ).astype(BF16)

    arrived(near_copies)
    for p in range(ND):
        expand(p, near_in[:, p])
    spread[0, d] = local_ref[0]
    spread[1, d] = local_ref[1]
    flat = (rows_all, nb * block)
    s0, s1 = spread[0, :ND].reshape(flat), spread[1, :ND].reshape(flat)
    for h in (0, 1):
        table = rounded[:, takes[h]]
        npart[h] = (dot(s0, table) + dot(s1, table)).reshape(4, 4, sel_dev, half)
    near_run = Plane(links, npart).reduce(nland)
    next(near_run)
    arrived(far_copies)
    for p in range(NG):
        expand(ND + p, far_in[:, p])
    flat = (cols_all, nb * block)
    s0, s1 = spread[0, ND:].reshape(flat), spread[1, ND:].reshape(flat)
    fpart[...] = (dot(s0, rounded[...]) + dot(s1, rounded[...])).reshape(4, 2, sel_dev, feat)
    far_run = Line(links, fpart).reduce(fpair, fsmall)
    next(far_run)
    next(near_run)
    next(far_run)
    next(near_run)
    together(near_run, far_run, text_run)

    far_sum = fpart[x, c]
    for h in (0, 1):
        chosen[:, takes[h]] = chosen0[:, takes[h]] + npart[h, y, z] + far_sum[:, takes[h]]
    picked = chosen[...]
    picked_parts = split(picked)
    before = dot3(picked_parts, (wh[...], wl[...]))
    curve = 0.5 * (1.0 + lax.erf(before * ROOT_HALF))
    hidden = before * curve
    node_norm = jnp.sqrt(jnp.sum(hidden * hidden, axis=1, keepdims=True) + EPS)
    unit_nodes = hidden / node_norm
    for h in (0, 1):
        units[h, y, z] = unit_nodes[:, takes[h]]
    unit_run = Plane(links, units).gather()
    next(unit_run)
    col_parts = split(cols[...].reshape(cols_all, feat))
    text_halves = [tuple(v[:, takes[h]] for v in col_parts) for h in (0, 1)]
    next(unit_run)
    next(unit_run)
    lane = lax.broadcasted_iota(jnp.int32, (8, cols_all), 1)
    ids = ((lane // sel_dev * ND + d) * sel_dev + lane % sel_dev)[:1]
    tags = near_in[2].reshape(rows_all, block).astype(F32)
    target = (tags[:, 1:2] * 64.0 + tags[:, 2:3] == ids.astype(F32)).astype(F32)
    wide = jnp.concatenate(
        [v.astype(F32) for v in (*picked_parts, picked_parts[0])] + [jnp.zeros_like(picked)], axis=0
    )
    slices_out[...] = wide.T.astype(BF16).reshape(slices_out.shape)
    slices[d] = slices_out[d]
    together(unit_run)
    slice_copies = links.all_dev(lambda e: slices_out.at[e], slices.at[d])

    unit_parts = [split(units[h].reshape(rows_all, half)) for h in (0, 1)]
    scores = dot3(unit_parts[0], text_halves[0], 1, 1) + dot3(unit_parts[1], text_halves[1], 1, 1)
    scores = SCALE * scores
    exps = jnp.exp(scores)
    row_in[d] = to_lanes(jnp.sum(exps, axis=1, keepdims=True))
    row_copies = links.all_dev(lambda e: row_in.at[d], row_in.at[d])
    col_sum = jnp.sum(exps, axis=0, keepdims=True)
    col_in[g] = jnp.broadcast_to(col_sum, (8, cols_all))
    col_copies = links.all_grp(lambda e: col_in.at[g], col_in.at[g])
    positive = jnp.sum(jnp.sum(target * scores, axis=1, keepdims=True), axis=0, keepdims=True)
    arrived(col_copies)
    col_total = jnp.sum(col_in[...], axis=0)[:1]
    arrived(row_copies)
    row_total = as_row(jnp.sum(row_in[...], axis=0), rows_all)
    row_recip = jnp.broadcast_to(1.0 / row_total, (128, rows_all)).T[:, :1]
    col_recip = 1.0 / col_total
    slope = 0.5 * exps * (row_recip + col_recip) - target
    slope_parts = split(slope)
    for h in (0, 1):
        spart[h] = dot3(slope_parts, text_halves[h]).reshape(4, 4, sel_dev, half)
    node_run = Plane(links, spart).reduce(sland)
    next(node_run)
    log_rows = jnp.sum(jnp.log(row_total), axis=1, keepdims=True)
    log_cols = jnp.sum(jnp.log(col_total), axis=1, keepdims=True)
    part = (log_rows / ND + log_cols / NG) / (2.0 * total_sel) - positive / total_sel
    loss_dev[d] = jnp.broadcast_to(part, (8, 128))
    for h in (0, 1):
        grown = dot3(slope_parts, unit_parts[h], 0, 0)
        tpart[:, :, :, takes[h]] = grown.reshape(4, 2, sel_dev, half)
    next(node_run)
    text_run = Line(links, tpart).reduce(tpair, tsmall)
    next(text_run)
    loss_copies = links.all_dev(lambda e: loss_dev.at[d], loss_dev.at[d])
    next(node_run)
    together(node_run, text_run)

    node_dir = SCALE * jnp.concatenate([spart[0, y, z], spart[1, y, z]], axis=1)
    node_back = (
        node_dir - unit_nodes * jnp.sum(unit_nodes * node_dir, axis=1, keepdims=True)
    ) / node_norm
    pre_grad = node_back * (curve + before * jnp.exp(-0.5 * before * before) * INV_ROOT_TWO_PI)
    for h in (0, 1):
        pre_all[h, y, z] = pre_grad[:, takes[h]]
    pre_run = Plane(links, pre_all).gather()
    next(pre_run)
    row_grads = dot3(split(pre_grad), (wh[...], wl[...]), 1, 1)
    g_far[x, c] = row_grads.astype(BF16)
    far_run = Line(links, g_far).gather()
    next(far_run)
    next(pre_run)
    arrived(loss_copies)
    loss_grp[g] = jnp.sum(loss_dev[...], axis=0)
    loss_copies = links.all_grp(lambda e: loss_grp.at[g], loss_grp.at[g])
    next(pre_run)
    next(far_run)
    some = 128 // sel_dev
    for q in (0, 1):
        for i in range(NPEER // some):
            rows = spread[q, i * some : (i + 1) * some].reshape(128, nb * block)
            spread_t[q, :, i * 128 : (i + 1) * 128] = rows.astype(F32).T.astype(BF16)
    next(pre_run)
    arrived(slice_copies)
    together(pre_run, far_run)

    pre_parts = []
    for h in (0, 1):
        hi, lo = split(pre_all[h].reshape(rows_all, half))
        pre_parts.append((hi, lo))
        for i, v in enumerate((hi, hi, lo, hi)):
            pre_stack[h, :, i] = v.reshape(ND, sel_dev, half)
        piece = 0.0
        for p in range(ND):
            piece += dot(slices[p], pre_stack[h, p].reshape(4 * sel_dev, half))
        gpart[:, h] = piece.reshape(2, piece.shape[0] // 2, half)
    core_copy = links.core(gpart.at[1 - c], gpair)
    group_grads = dot3(pre_parts[0], (wh[:, takes[0]], wl[:, takes[0]]), 1, 1)
    group_grads += dot3(pre_parts[1], (wh[:, takes[1]], wl[:, takes[1]]), 1, 1)
    group_grads = group_grads.astype(BF16)
    core_copy.wait_recv()
    gx[x] = gpart[c] + gpair[...]
    copies = [links.shift(gx.at[x], gx.at[x], "x", i) for i in (1, 2, 3)]

    spot = lax.broadcasted_iota(jnp.int32, (sel_dev, nodes_dev), 1)
    hot = (spot_ref[:, :1] == spot).astype(F32).astype(BF16)
    top, mid = split(row_grads)
    low = (row_grads - top.astype(F32) - mid.astype(F32)).astype(BF16)

    def node_grads(h):
        take = takes[h]
        near = group_grads[:, take]
        far = g_far[:, :, :, take].reshape(cols_all, half)
        total = dot(spread_t[0, :, :rows_all], near) + dot(spread_t[1, :, :rows_all], near)
        total += dot(spread_t[0, :, rows_all:], far) + dot(spread_t[1, :, rows_all:], far)
        total += dot(hot, top[:, take], 0, 0) + dot(hot, mid[:, take], 0, 0)
        gn_ref[:, take] = total + dot(hot, low[:, take], 0, 0)

    node_grads(0)
    arrived(copies)
    gfull[c, :, y, z] = gx[0] + gx[1] + gx[2] + gx[3]
    crossings = []
    weight_run = Plane(links, gfull.at[c]).gather(lambda view: crossings.append(links.core(view, view)))
    next(weight_run)
    node_grads(1)
    next(weight_run)
    text_dir = SCALE * tpart[x, c]
    gt_ref[...] = (
        text_dir - unit_texts * jnp.sum(unit_texts * text_dir, axis=1, keepdims=True)
    ) / text_norm
    arrived(loss_copies)
    loss_ref[...] = jnp.sum(loss_grp[...], axis=0)[:1, :1]
    together(weight_run)
    arrived(crossings)
    deep = gfull.shape[4]
    for e in range(ND):
        for core in (0, 1):
            for h in (0, 1):
                start = (2 * e + core) * deep
                gw_ref[start : start + deep, takes[h]] = gfull[core, h, e // 4, e % 4]
    for copy in links.copies:
        copy.wait_send()


def shards(node_features, tiles, tile_list, weight, texts, selected, pairing):
    device = lax.axis_index("grp") * ND + lax.axis_index("dev")
    tile_dev, block = tiles.shape[0], tiles.shape[1]
    nodes_dev, feat = node_features.shape
    sel_dev = selected.shape[0]
    nb = nodes_dev // block
    half = feat // 2
    deep = feat // 32
    my_list = lax.dynamic_slice_in_dim(tile_list, device * tile_dev, tile_dev, 0).reshape(-1)
    vmem = pl.BlockSpec(memory_space=pltpu.VMEM)
    smem = pl.BlockSpec(memory_space=pltpu.SMEM)
    made = pl.pallas_call(
        prep_kernel,
        out_shape=(
            jax.ShapeDtypeStruct((3, NPEER + 1, sel_dev, block), BF16),
            jax.ShapeDtypeStruct((2, sel_dev, nb * block), BF16),
            jax.ShapeDtypeStruct((nodes_dev, feat), BF16),
            jax.ShapeDtypeStruct((sel_dev, feat), F32),
            jax.ShapeDtypeStruct((sel_dev, block), jnp.int32),
        ),
        in_specs=[smem, smem, smem, vmem, vmem],
        out_specs=(vmem,) * 5,
        scratch_shapes=[
            pltpu.VMEM((nb, sel_dev, block), F32),
            pltpu.VMEM((nb, sel_dev, block), BF16),
            pltpu.VMEM((sel_dev, block), jnp.int32),
            pltpu.SMEM((NPEER + 1,), jnp.int32),
            pltpu.SMEM((NPEER + 1,), jnp.int32),
        ],
        compiler_params=pltpu.CompilerParams(vmem_limit_bytes=24 * 2**20),
    )(my_list, selected, pairing, tiles, node_features)

    def f32(*shape):
        return pltpu.VMEM(shape, F32)

    def bf16(*shape):
        return pltpu.VMEM(shape, BF16)

    plane = f32(2, 4, 4, sel_dev, half)
    landing = f32(2, 15, sel_dev, half)
    line = [f32(4, 2, sel_dev, feat), f32(4, sel_dev, feat), f32(2, 16 + sel_dev, feat)]
    loss, grad_nodes, grad_weight, grad_texts = pl.pallas_call(
        main_kernel,
        out_shape=(
            jax.ShapeDtypeStruct((1, 1), F32),
            jax.ShapeDtypeStruct((nodes_dev, feat), F32),
            jax.ShapeDtypeStruct((feat, feat), F32),
            jax.ShapeDtypeStruct((sel_dev, feat), F32),
        ),
        in_specs=[vmem] * 7,
        out_specs=(vmem,) * 4,
        scratch_shapes=[
            bf16(3, ND, sel_dev, block),
            bf16(3, NG, sel_dev, block),
            bf16(2, NPEER, sel_dev, nb * block),
            bf16(2, nb * block, NPEER * sel_dev),
            bf16(feat, feat),
            bf16(feat, feat),
            plane, landing, *line,
            plane, f32(4, 2, sel_dev, feat),
            plane, landing, *line,
            f32(ND, 8, 128),
            f32(NG, 8, NG * sel_dev),
            f32(ND, 8, 128),
            f32(NG, 8, 128),
            bf16(ND, 2 * deep, 4 * sel_dev),
            bf16(ND, 2 * deep, 4 * sel_dev),
            plane,
            bf16(2, ND, 4, sel_dev, half),
            bf16(4, 2, sel_dev, feat),
            f32(2, 2, deep, half),
            f32(2, deep, half),
            f32(4, 2, deep, half),
            f32(2, 2, 4, 4, deep, half),
            f32(sel_dev, feat),
            pltpu.SemaphoreType.DMA((SEMS,)),
            pltpu.SemaphoreType.DMA((SEMS,)),
        ],
        compiler_params=pltpu.CompilerParams(
            collective_id=0, has_side_effects=True, vmem_limit_bytes=60 * 2**20
        ),
    )(*made, weight, texts)
    return loss.reshape(()), grad_nodes, grad_weight, grad_texts


def solution(mesh):
    both = ("grp", "dev")
    placed = (
        P(both, None),
        P(both, None, None),
        P(),
        P(),
        P(both, None),
        P(both),
        P(both),
    )
    return jax.shard_map(
        shards,
        mesh=mesh,
        in_specs=placed,
        out_specs=(P(), P(both, None), P(), P(both, None)),
        check_vma=False,
    )
```

time: 152 us -> 148 us (0.974)
  Pallas kernels: 138 us -> 131 us
  local copies, waits for them, and re-layouts: 11.5 us -> 13.5 us
  between operations: 0.7 us -> 2.6 us
  other arithmetic: 1.82 us -> 0 us
    pallas_call x1, Pallas kernels: 136 us -> 129 us  [shards(): pl.pallas_call(main_kernel, out_shape=(jax.ShapeDtypeStruct((1, 1), F32),...]
    unnamed x17 -> x27, local copies, waits for them, and re-layouts: 8.41 us -> 13.2 us
where the time goes in v2:
time: 148 us; the launch traced here: 147 us
  Pallas kernels  131 us (89%)
  local copies, waits for them, and re-layouts  13.5 us (9%)
  between operations  2.6 us (2%)
    pallas_call x1, Pallas kernels, shards(): pl.pallas_call(main_kernel, out_shape=(jax.ShapeDtypeStruct((1, 1), F32),...  129 us
    unnamed x27, local copies, waits for them, and re-layouts  13.2 us

profile of v2, /device:TPU:1, one launch (start us, length us, event | category | flops | bytes accessed | tf_op | source)
XLA Modules:
  0.0 147.4 jit_solution(1792579257178626752)
XLA Ops:
  0.6 0.0 copy-start
  0.7 0.8 copy-done
  1.4 0.1 constant_dynamic-slice_fusion
  1.5 0.1 copy.12
  1.6 0.1 reshape.14.list_ref
  1.8 0.0 copy-start.1
  1.8 1.4 copy-done.1
  3.2 0.0 copy-start.2
  3.2 1.4 copy-done.2
  4.6 0.0 copy-start.8
  4.6 0.7 copy-done.8
  5.3 0.0 copy-start.9
  5.3 0.7 copy-done.9
  5.9 1.8 %shard_map.102 = (bf16[3,25,32,128]{3,2,1,0:T(8,128)(2,1)S(1)}, bf16[2,32,512]{2,1,0:T(8,128)(2,1)S(1)}, bf16[512,768]{1,0:T(8,128)(2,1)S(1)}, f32[32,768]{1,0:T(8,128)S(1)}, s32[32,128]{1,0:T(8,128)S(1)}) custom-call(s32[104]{0:T(128)S(1)} %reshape.14.list_ref, s32[32]{0:T(128)S(1)} %copy-done.8, s32[32]{0:T(128)S(1)} %copy-done.9, ...), custom_call_target="tpu_custom_call" | custom-call | tf_op jit(solution)/shard_map/pallas_call | solution.py:608
  7.8 0.0 copy-start.3
  7.8 0.9 copy-done.3
  8.6 0.0 copy-start.4
  8.6 0.8 copy-done.4
  9.5 0.0 copy-start.5
  9.5 0.6 copy-done.5
  10.1 0.0 copy-start.6
  10.1 0.6 copy-done.6
  10.7 0.0 copy-start.7
  10.7 0.6 copy-done.7
  11.3 129.5 %shard_map.103 = (f32[1,1]{1,0:T(1,128)}, f32[512,768]{1,0:T(8,128)}, f32[768,768]{1,0:T(8,128)}, f32[32,768]{1,0:T(8,128)}) custom-call(bf16[3,25,32,128]{3,2,1,0:T(8,128)(2,1)} %copy-done.4, bf16[2,32,512]{2,1,0:T(8,128)(2,1)} %copy-done.6, bf16[512,768]{1,0:T(8,128)(2,1)} %copy-done.3, f32[32,768]{1,0:T(8,128)} %copy-done.5, s32[32,128]{1,0:T(8,128)} %copy-done.7, ...), custom_call_target="tpu_custom_call" | custom-call | tf_op jit(solution)/shard_map/pallas_call | solution.py:638
  140.8 0.0 copy-start.10
  141.6 2.7 %copy.18 = f32[512,768]{1,0:T(8,128)} copy(f32[512,768]{1,0:T(8,128)} %get-tuple-element.27) | data formatting | bytes 3145728
  144.2 0.0 copy-done.10
  144.2 0.0 copy-start.11
  144.2 1.4 copy.19
  145.6 0.0 copy-done.11
  145.6 0.6 copy.20
Async XLA Ops:
  0.6 0.8 copy-start
  1.8 1.5 copy-start.1
  3.2 1.4 copy-start.2
  4.6 0.7 copy-start.8
  5.3 0.7 copy-start.9
  7.8 0.9 copy-start.3
  8.6 0.8 copy-start.4
  9.5 0.6 copy-start.5
  10.1 0.6 copy-start.6
  10.7 0.6 copy-start.7
  140.8 3.4 %copy-start.10 = (f32[768,768]{1,0:T(8,128)S(1)}, f32[768,768]{1,0:T(8,128)}, u32[]{:S(2)}) copy-start(f32[768,768]{1,0:T(8,128)} %get-tuple-element.28) | copy-start | bytes 7077892
  144.2 1.4 copy-start.11

commit v3 on v2

--- a/solution.py
+++ b/solution.py
@@ -142,62 +142,6 @@
         copy.wait_recv()
 
 
-class Ring:
-    def __init__(self, links, axis, chunk):
-        self.links, self.axis, self.chunk = links, axis, chunk
-        r = links.pos(axis)
-        self.r, self.up, self.down, self.far = r, (r + 1) % 4, (r + 3) % 4, (r + 2) % 4
-
-    def gather_1(self):
-        own = self.chunk(self.r, None)
-        self.a = self.links.shift(own, own, self.axis, 1)
-        self.b = self.links.shift(own, own, self.axis, 3)
-
-    def gather_2(self):
-        self.a.wait_recv()
-        part = self.chunk(self.down, 0)
-        self.a = self.links.shift(part, part, self.axis, 1)
-        self.b.wait_recv()
-        part = self.chunk(self.up, 1)
-        self.b = self.links.shift(part, part, self.axis, 3)
-
-    def gather_3(self):
-        self.a.wait_recv()
-        self.b.wait_recv()
-
-    def reduce_1(self, land):
-        self.land = land
-        send = self.links.shift
-        self.a = send(self.chunk(self.far, 0), land(0, 0, 0), self.axis, 1)
-        self.b = send(self.chunk(self.far, 1), land(0, 1, 1), self.axis, 3)
-        self.a1 = send(self.chunk(self.up, 1), land(1, 0, 1), self.axis, 1)
-        self.b1 = send(self.chunk(self.down, 0), land(1, 1, 0), self.axis, 3)
-
-    def reduce_2(self):
-        send, land = self.links.shift, self.land
-        self.a.wait_recv()
-        view = self.chunk(self.up, 0)
-        view[...] += land(0, 0, 0)[...]
-        self.a = send(view, land(1, 0, 0), self.axis, 1)
-        self.b.wait_recv()
-        view = self.chunk(self.down, 1)
-        view[...] += land(0, 1, 1)[...]
-        self.b = send(view, land(1, 1, 1), self.axis, 3)
-
-    def reduce_3(self):
-        arrived([self.a, self.b, self.a1, self.b1])
-        for s in (0, 1):
-            view = self.chunk(self.r, s)
-            view[...] += self.land(1, 0, s)[...] + self.land(1, 1, s)[...]
-
-
-def rows_of(ref, s, cut):
-    if s is None:
-        return ref
-    n = ref.shape[0]
-    return ref.at[pl.ds(0, cut)] if s == 0 else ref.at[pl.ds(cut, n - cut)]
-
-
 class Plane:
     def __init__(self, links, buf):
         self.links, self.buf = links, buf
@@ -206,142 +150,103 @@
     def at(self, h, out, into):
         links = self.links
         out = (links.pos(self.outer[h]) + out) % 4
+        if into is None:
+            return self.buf.at[0, out] if h == 0 else self.buf.at[1, :, out]
         into = (links.pos(self.inner[h]) + into) % 4
         return self.buf.at[0, out, into] if h == 0 else self.buf.at[1, into, out]
 
-    def gather(self, relay=lambda view: None):
+    def gather(self, cross=None):
         shift, at, outer, inner = self.links.shift, self.at, self.outer, self.inner
-        halves = (0, 1)
-        first, far, out, onward = {}, {}, {}, {}
+        near, away = {}, {}
 
         def send_out(h, o):
             view = at(h, 0, o)
-            out[h, o] = shift(view, view, outer[h], 1), shift(view, view, outer[h], 3)
-            relay(view)
-
-        def landed(h, o):
-            for k, side in ((0, 3), (1, 1)):
-                out[h, o][k].wait_recv()
-                view = at(h, side, o)
-                if (o in (0, 3)) == (side == 3):
-                    onward[h, o] = shift(view, view, outer[h], 1 if side == 3 else 3)
-                relay(view)
-
-        for h in halves:
+            for i in (2, 1, 3):
+                away[h, i, o] = shift(view, view, outer[h], i)
+
+        for h in (0, 1):
             view = at(h, 0, 0)
-            first[h] = shift(view, view, inner[h], 1), shift(view, view, inner[h], 3)
-        for h in halves:
+            for i in (2, 1, 3):
+                near[h, i] = shift(view, view, inner[h], i)
+        for h in (0, 1):
             send_out(h, 0)
         yield
-        for h in halves:
-            first[h][0].wait_recv()
-            view = at(h, 0, 3)
-            far[h] = shift(view, view, inner[h], 1)
-            send_out(h, 3)
-            first[h][1].wait_recv()
-            send_out(h, 1)
-        yield
-        for h in halves:
-            landed(h, 0)
-        for h in halves:
-            far[h].wait_recv()
-            send_out(h, 2)
-        yield
-        for o in (3, 1):
-            for h in halves:
-                landed(h, o)
-        yield
-        for h in halves:
-            landed(h, 2)
-        yield
-        for o in (0, 3, 1, 2):
-            for h in halves:
-                onward[h, o].wait_recv()
-                relay(at(h, 2, o))
+        for i in (2, 1, 3):
+            for h in (0, 1):
+                near[h, i].wait_recv()
+                send_out(h, 4 - i)
+        if cross:
+            for h in (0, 1):
+                cross(at(h, 0, None))
+        yield
+        for i in (2, 1, 3):
+            for h in (0, 1):
+                for o in (0, 2, 3, 1):
+                    away[h, i, o].wait_recv()
+                if cross:
+                    cross(at(h, 4 - i, None))
         yield
 
     def reduce(self, land):
         shift, at, outer, inner = self.links.shift, self.at, self.outer, self.inner
-        order = (2, 3, 1, 0)
-        early, direct, late, last = {}, {}, {}, {}
-
-        def way(o):
-            return 1 if o in (2, 3) else 3
-
+        order = (2, 1, 3, 0)
+        away, near = {}, {}
         for o in order:
             for h in (0, 1):
-                w = way(o)
-                early[h, o] = shift(at(h, 2, o), land.at[h, o], outer[h], w)
-                direct[h, o] = shift(at(h, 4 - w, o), land.at[h, 4 + o], outer[h], 4 - w)
+                for i in (2, 1, 3):
+                    away[h, i, o] = shift(at(h, i, o), land.at[h, 4 * (i - 1) + o], outer[h], i)
         yield
         for o in order:
             for h in (0, 1):
-                w = way(o)
-                early[h, o].wait_recv()
-                view = at(h, w, o)
-                view[...] += land[h, o]
-                late[h, o] = shift(view, land.at[h, 8 + o], outer[h], w)
-            if o == 3:
-                yield
-        yield
-        for o in order:
-            for h in (0, 1):
-                direct[h, o].wait_recv()
-                late[h, o].wait_recv()
+                for i in (2, 1, 3):
+                    away[h, i, o].wait_recv()
                 view = at(h, 0, o)
-                total = view[...] + land[h, 4 + o] + land[h, 8 + o]
-                if o == 1:
-                    last[h, 2].wait_recv()
-                    total += land[h, 12]
-                view[...] = total
-                if o == 2:
-                    last[h, 2] = shift(view, land.at[h, 12], inner[h], 1)
-                if o == 3:
-                    last[h, 3] = shift(view, land.at[h, 14], inner[h], 3)
-                if o == 1:
-                    last[h, 1] = shift(view, land.at[h, 13], inner[h], 1)
+                view[...] += land[h, o] + land[h, 4 + o] + land[h, 8 + o]
+                if o:
+                    near[h, o] = shift(view, land.at[h, 11 + o], inner[h], o)
             yield
         for h in (0, 1):
-            last[h, 1].wait_recv()
-            last[h, 3].wait_recv()
+            for o in (2, 1, 3):
+                near[h, o].wait_recv()
             view = at(h, 0, 0)
-            view[...] += land[h, 13] + land[h, 14]
+            view[...] += land[h, 12] + land[h, 13] + land[h, 14]
         yield
 
 
 class Line:
     def __init__(self, links, buf):
-        c = links.c
         self.links, self.buf = links, buf
-        self.ring = Ring(links, "x", lambda i, s: rows_of(buf.at[i, c], s, 16))
 
     def gather(self):
-        for name in ("gather_1", "gather_2", "gather_3"):
-            getattr(self.ring, name)()
-            yield
-        view = self.buf.at[:, self.links.c]
-        copy = self.links.core(view, view)
+        links = self.links
+        x, c = links.x, links.c
+        own = self.buf.at[x, c]
+        ways = [links.shift(own, own, "x", i) for i in (2, 1, 3)]
+        crossed = [links.core(own, own)]
+        yield
+        for i, way in zip((2, 1, 3), ways):
+            way.wait_recv()
+            view = self.buf.at[(x + 4 - i) % 4, c]
+            crossed.append(links.core(view, view))
+        yield
+        arrived(crossed)
+        yield
+
+    def reduce(self, pair, land):
+        links = self.links
+        x, c = links.x, links.c
+        copy = links.core(self.buf.at[:, 1 - c], pair)
         yield
         copy.wait_recv()
-        yield
-
-    def reduce(self, pair, small):
-        rows = self.buf.shape[2]
-
-        def land(k, way, s):
-            n = (16, rows - 16)[s]
-            return small.at[way, pl.ds(0 if k == 0 else (16 if s == 0 else 32), n)]
-
-        copy = self.links.core(self.buf.at[:, 1 - self.links.c], pair)
-        yield
-        copy.wait_recv()
-        view = self.buf.at[:, self.links.c]
+        view = self.buf.at[:, c]
         view[...] += pair[...]
-        self.ring.reduce_1(land)
-        yield
-        self.ring.reduce_2()
-        yield
-        self.ring.reduce_3()
+        ways = [
+            links.shift(self.buf.at[(x + i) % 4, c], land.at[i - 1], "x", i) for i in (2, 1, 3)
+        ]
+        yield
+        arrived(ways)
+        view = self.buf.at[x, c]
+        view[...] += land[0] + land[1] + land[2]
         yield
 
 
@@ -437,9 +342,7 @@
     fpart[...] = (dot(s0, rounded[...]) + dot(s1, rounded[...])).reshape(4, 2, sel_dev, feat)
     far_run = Line(links, fpart).reduce(fpair, fsmall)
     next(far_run)
-    next(near_run)
     next(far_run)
-    next(near_run)
     together(near_run, far_run, text_run)
 
     far_sum = fpart[x, c]
@@ -458,7 +361,6 @@
     next(unit_run)
     col_parts = split(cols[...].reshape(cols_all, feat))
     text_halves = [tuple(v[:, takes[h]] for v in col_parts) for h in (0, 1)]
-    next(unit_run)
     next(unit_run)
     lane = lax.broadcasted_iota(jnp.int32, (8, cols_all), 1)
     ids = ((lane // sel_dev * ND + d) * sel_dev + lane % sel_dev)[:1]
@@ -470,7 +372,6 @@
     slices_out[...] = wide.T.astype(BF16).reshape(slices_out.shape)
     slices[d] = slices_out[d]
     together(unit_run)
-    slice_copies = links.all_dev(lambda e: slices_out.at[e], slices.at[d])
 
     unit_parts = [split(units[h].reshape(rows_all, half)) for h in (0, 1)]
     scores = dot3(unit_parts[0], text_halves[0], 1, 1) + dot3(unit_parts[1], text_halves[1], 1, 1)
@@ -481,6 +382,7 @@
     col_sum = jnp.sum(exps, axis=0, keepdims=True)
     col_in[g] = jnp.broadcast_to(col_sum, (8, cols_all))
     col_copies = links.all_grp(lambda e: col_in.at[g], col_in.at[g])
+    slice_copies = links.all_dev(lambda e: slices_out.at[e], slices.at[d])
     positive = jnp.sum(jnp.sum(target * scores, axis=1, keepdims=True), axis=0, keepdims=True)
     arrived(col_copies)
     col_total = jnp.sum(col_in[...], axis=0)[:1]
@@ -501,11 +403,9 @@
     for h in (0, 1):
         grown = dot3(slope_parts, unit_parts[h], 0, 0)
         tpart[:, :, :, takes[h]] = grown.reshape(4, 2, sel_dev, half)
-    next(node_run)
     text_run = Line(links, tpart).reduce(tpair, tsmall)
     next(text_run)
     loss_copies = links.all_dev(lambda e: loss_dev.at[d], loss_dev.at[d])
-    next(node_run)
     together(node_run, text_run)
 
     node_dir = SCALE * jnp.concatenate([spart[0, y, z], spart[1, y, z]], axis=1)
@@ -522,17 +422,15 @@
     far_run = Line(links, g_far).gather()
     next(far_run)
     next(pre_run)
+    next(far_run)
     arrived(loss_copies)
     loss_grp[g] = jnp.sum(loss_dev[...], axis=0)
     loss_copies = links.all_grp(lambda e: loss_grp.at[g], loss_grp.at[g])
-    next(pre_run)
-    next(far_run)
     some = 128 // sel_dev
     for q in (0, 1):
         for i in range(NPEER // some):
             rows = spread[q, i * some : (i + 1) * some].reshape(128, nb * block)
             spread_t[q, :, i * 128 : (i + 1) * 128] = rows.astype(F32).T.astype(BF16)
-    next(pre_run)
     arrived(slice_copies)
     together(pre_run, far_run)
 
@@ -574,8 +472,8 @@
     crossings = []
     weight_run = Plane(links, gfull.at[c]).gather(lambda view: crossings.append(links.core(view, view)))
     next(weight_run)
+    next(weight_run)
     node_grads(1)
-    next(weight_run)
     text_dir = SCALE * tpart[x, c]
     gt_ref[...] = (
         text_dir - unit_texts * jnp.sum(unit_texts * text_dir, axis=1, keepdims=True)
@@ -623,7 +521,7 @@
             pltpu.SMEM((NPEER + 1,), jnp.int32),
             pltpu.SMEM((NPEER + 1,), jnp.int32),
         ],
-        compiler_params=pltpu.CompilerParams(vmem_limit_bytes=24 * 2**20),
+        compiler_params=pltpu.CompilerParams(vmem_limit_bytes=60 * 2**20),
     )(my_list, selected, pairing, tiles, node_features)
 
     def f32(*shape):
@@ -634,7 +532,7 @@
 
     plane = f32(2, 4, 4, sel_dev, half)
     landing = f32(2, 15, sel_dev, half)
-    line = [f32(4, 2, sel_dev, feat), f32(4, sel_dev, feat), f32(2, 16 + sel_dev, feat)]
+    line = [f32(4, 2, sel_dev, feat), f32(4, sel_dev, feat), f32(3, sel_dev, feat)]
     loss, grad_nodes, grad_weight, grad_texts = pl.pallas_call(
         main_kernel,
         out_shape=(

time: 148 us -> 128 us (0.86)
  Pallas kernels: 131 us -> 119 us
  local copies, waits for them, and re-layouts: 13.5 us -> 6.33 us
    pallas_call x1, Pallas kernels: 129 us -> 114 us  [shards(): pl.pallas_call(main_kernel, out_shape=(jax.ShapeDtypeStruct((1, 1), F32),...]
    unnamed x27 -> x9, local copies, waits for them, and re-layouts: 13.2 us -> 5.51 us
    pallas_call x1, Pallas kernels: 1.82 us -> 4.24 us  [shards(): pl.pallas_call(prep_kernel, out_shape=(jax.ShapeDtypeStruct((3, NPEER + 1...]
where the time goes in v3:
time: 128 us
  Pallas kernels  119 us (93%)
  local copies, waits for them, and re-layouts  6.33 us (5%)
  between operations  2.56 us (2%)
    pallas_call x1, Pallas kernels, shards(): pl.pallas_call(main_kernel, out_shape=(jax.ShapeDtypeStruct((1, 1), F32),...  114 us
    unnamed x9, local copies, waits for them, and re-layouts  5.51 us
    pallas_call x1, Pallas kernels, shards(): pl.pallas_call(prep_kernel, out_shape=(jax.ShapeDtypeStruct((3, NPEER + 1...  4.24 us

profile of v3, /device:TPU:1, one launch (start us, length us, event | category | flops | bytes accessed | tf_op | source)
XLA Modules:
  0.0 127.6 jit_solution(6797669185066897541)
XLA Ops:
  0.6 0.0 copy-start
  0.7 0.8 copy-done
  1.4 0.1 constant_dynamic-slice_fusion
  1.5 0.1 copy.12
  1.6 0.6 reshape.14.list_ref
  2.3 4.2 %shard_map.102 = (bf16[3,25,32,128]{3,2,1,0:T(8,128)(2,1)}, bf16[2,32,512]{2,1,0:T(8,128)(2,1)}, bf16[512,768]{1,0:T(8,128)(2,1)}, f32[32,768]{1,0:T(8,128)}, s32[32,128]{1,0:T(8,128)}) custom-call(s32[104]{0:T(128)} %reshape.14.list_ref, s32[32]{0:T(128)} %sel_ref.1, s32[32]{0:T(128)} %pair_ref.1, bf16[52,128,128]{2,1,0:T(8,128)(2,1)} %tiles_ref.1, ...), custom_call_target="tpu_custom_call" | custom-call | tf_op jit(solution)/shard_map/pallas_call | solution.py:506
  6.5 114.4 %shard_map.103 = (f32[1,1]{1,0:T(1,128)}, f32[512,768]{1,0:T(8,128)}, f32[768,768]{1,0:T(8,128)}, f32[32,768]{1,0:T(8,128)}) custom-call(bf16[3,25,32,128]{3,2,1,0:T(8,128)(2,1)} %get-tuple-element.13.rows_ref, bf16[2,32,512]{2,1,0:T(8,128)(2,1)} %get-tuple-element.14.local_ref, bf16[512,768]{1,0:T(8,128)(2,1)} %get-tuple-element.15.rounded, ...), custom_call_target="tpu_custom_call" | custom-call | tf_op jit(solution)/shard_map/pallas_call | solution.py:536
  120.9 0.0 copy-start.1
  121.7 2.7 %copy.18 = f32[512,768]{1,0:T(8,128)} copy(f32[512,768]{1,0:T(8,128)} %get-tuple-element.27) | data formatting | bytes 3145728
  124.4 0.0 copy-done.1
  124.4 0.0 copy-start.2
  124.4 1.4 %copy.19 = f32[768,768]{1,0:T(8,128)} copy(f32[768,768]{1,0:T(8,128)S(1)} %copy-done.1) | data formatting | bytes 4718592
  125.8 0.0 copy-done.2
  125.8 0.6 copy.20
Async XLA Ops:
  0.6 0.8 copy-start
  120.9 3.4 %copy-start.1 = (f32[768,768]{1,0:T(8,128)S(1)}, f32[768,768]{1,0:T(8,128)}, u32[]{:S(2)}) copy-start(f32[768,768]{1,0:T(8,128)} %get-tuple-element.28) | copy-start | bytes 7077892
  124.4 1.4 %copy-start.2 = (f32[32,768]{1,0:T(8,128)S(1)}, f32[32,768]{1,0:T(8,128)}, u32[]{:S(2)}) copy-start(f32[32,768]{1,0:T(8,128)} %get-tuple-element.29) | copy-start | bytes 294916

commit v4 on v3

--- a/solution.py
+++ b/solution.py
@@ -34,23 +34,28 @@
 
 
 def prep_kernel(
-    list_ref, sel_ref, pair_ref, tiles_ref, nodes_ref,
-    rows_ref, local_ref, rounded_ref, chosen_ref, spot_ref,
-    acc, onehot, column, count, meta,
+    list_ref, sel_ref, pair_ref, tiles_ref,
+    rows_ref, local_ref, spot_ref, own_ref,
+    acc, onehot, column, count, meta, window, sem,
 ):
     g, d = lax.axis_index("grp"), lax.axis_index("dev")
     device = g * ND + d
     n_tiles, block = tiles_ref.shape[0], tiles_ref.shape[1]
+    wide = window.shape[1]
+    first = jnp.minimum(device * n_tiles // 128 * 128, list_ref.shape[1] - wide)
+    first = pl.multiple_of(first, 128)
+    fetch = pltpu.make_async_copy(list_ref.at[:, pl.ds(first, wide)], window, sem)
+    fetch.start()
     sel_dev = sel_ref.shape[0]
-    nodes_dev = nodes_ref.shape[0]
-    nb = nodes_dev // block
+    nb = local_ref.shape[2] // block
+    nodes_dev = nb * block
     rows_ref[...] = jnp.zeros_like(rows_ref)
     acc[...] = jnp.zeros_like(acc)
     for k in range(sel_dev):
         own = sel_ref[k] - device * nodes_dev
+        own_ref[k] = own
         spot_ref[pl.ds(k, 1), :] = jnp.full((1, block), own, jnp.int32)
         column[pl.ds(k, 1), :] = jnp.full((1, block), pair_ref[k], jnp.int32)
-        chosen_ref[pl.ds(k, 1), :] = nodes_ref[pl.ds(own, 1), :]
     lane = lax.broadcasted_iota(jnp.int32, (sel_dev, block), 1)
     sel = spot_ref[...]
     for b in range(nb):
@@ -58,9 +63,11 @@
     for p in range(NPEER + 1):
         count[p] = 0
         meta[p] = 0
+    fetch.wait()
+    skip = device * n_tiles - first
     for t in range(n_tiles):
-        row_block = list_ref[2 * t] - device * nb
-        col = list_ref[2 * t + 1]
+        row_block = window[0, skip + t] - device * nb
+        col = window[1, skip + t]
         owner = col // nb
         col_block = col - owner * nb
         og = owner // ND
@@ -83,7 +90,6 @@
         hi, lo = split(acc[b])
         local_ref[0, :, b * block : (b + 1) * block] = hi
         local_ref[1, :, b * block : (b + 1) * block] = lo
-    rounded_ref[...] = nodes_ref[...].astype(BF16)
 
 
 class Links:
@@ -191,11 +197,11 @@
         shift, at, outer, inner = self.links.shift, self.at, self.outer, self.inner
         order = (2, 1, 3, 0)
         away, near = {}, {}
-        for o in order:
-            for h in (0, 1):
+        for h in (0, 1):
+            for o in order:
                 for i in (2, 1, 3):
                     away[h, i, o] = shift(at(h, i, o), land.at[h, 4 * (i - 1) + o], outer[h], i)
-        yield
+            yield
         for o in order:
             for h in (0, 1):
                 for i in (2, 1, 3):
@@ -268,20 +274,21 @@
 
 
 def main_kernel(
-    rows_ref, local_ref, rounded, chosen0, spot_ref, weight_ref, texts_ref,
-    loss_ref, gn_ref, gw_ref, gt_ref,
+    rows_ref, local_ref, spot_ref, own_ref, nodes_hbm, weight_hbm, texts_ref,
+    loss_ref, gn_out, gw_out, gt_ref,
+    nodes_ref, weight_ref, rounded, gn_ref,
     near_in, far_in, spread, spread_t, wh, wl,
     npart, nland, fpart, fpair, fsmall,
     units, cols, spart, sland, tpart, tpair, tsmall,
     row_in, col_in, loss_dev, loss_grp, slices_out, slices, pre_all, pre_stack, g_far,
     gpart, gpair, gx, gfull, chosen,
-    send_sem, recv_sem,
+    send_sem, recv_sem, local_sem,
 ):
     links = Links(send_sem, recv_sem)
     g, d, x, c, y, z = links.g, links.d, links.x, links.c, links.y, links.z
     sel_dev, feat = texts_ref.shape
     half = feat // 2
-    nodes_dev = rounded.shape[0]
+    nodes_dev = nodes_ref.shape[0]
     block = near_in.shape[3]
     nb = nodes_dev // block
     total_sel = sel_dev * NG * ND
@@ -294,6 +301,11 @@
         pl.semaphore_signal(barrier, inc=1, device_id=(g, (d + i) % ND), device_id_type=MESH)
     for i in range(1, NG):
         pl.semaphore_signal(barrier, inc=1, device_id=((g + i) % NG, d), device_id_type=MESH)
+
+    nodes_copy = pltpu.make_async_copy(nodes_hbm, nodes_ref, local_sem.at[0])
+    weight_copy = pltpu.make_async_copy(weight_hbm, weight_ref, local_sem.at[1])
+    nodes_copy.start()
+    weight_copy.start()
 
     texts = texts_ref[...]
     text_norm = jnp.sqrt(jnp.sum(texts * texts, axis=1, keepdims=True) + EPS)
@@ -308,6 +320,11 @@
     far_copies = links.all_grp(lambda e: rows_ref.at[:, ND + e], far_in.at[:, g])
     text_run = Line(links, cols).gather()
     next(text_run)
+    nodes_copy.wait()
+    rounded[...] = nodes_ref[...].astype(BF16)
+    for k in range(sel_dev):
+        chosen[pl.ds(k, 1), :] = nodes_ref[pl.ds(own_ref[k], 1), :]
+    weight_copy.wait()
     hi, lo = split(weight_ref[...])
     wh[...] = hi
     wl[...] = lo
@@ -329,11 +346,11 @@
     spread[1, d] = local_ref[1]
     flat = (rows_all, nb * block)
     s0, s1 = spread[0, :ND].reshape(flat), spread[1, :ND].reshape(flat)
+    near_run = Plane(links, npart).reduce(nland)
     for h in (0, 1):
         table = rounded[:, takes[h]]
         npart[h] = (dot(s0, table) + dot(s1, table)).reshape(4, 4, sel_dev, half)
-    near_run = Plane(links, npart).reduce(nland)
-    next(near_run)
+        next(near_run)
     arrived(far_copies)
     for p in range(NG):
         expand(ND + p, far_in[:, p])
@@ -347,7 +364,7 @@
 
     far_sum = fpart[x, c]
     for h in (0, 1):
-        chosen[:, takes[h]] = chosen0[:, takes[h]] + npart[h, y, z] + far_sum[:, takes[h]]
+        chosen[:, takes[h]] += npart[h, y, z] + far_sum[:, takes[h]]
     picked = chosen[...]
     picked_parts = split(picked)
     before = dot3(picked_parts, (wh[...], wl[...]))
@@ -392,10 +409,10 @@
     col_recip = 1.0 / col_total
     slope = 0.5 * exps * (row_recip + col_recip) - target
     slope_parts = split(slope)
+    node_run = Plane(links, spart).reduce(sland)
     for h in (0, 1):
         spart[h] = dot3(slope_parts, text_halves[h]).reshape(4, 4, sel_dev, half)
-    node_run = Plane(links, spart).reduce(sland)
-    next(node_run)
+        next(node_run)
     log_rows = jnp.sum(jnp.log(row_total), axis=1, keepdims=True)
     log_cols = jnp.sum(jnp.log(col_total), axis=1, keepdims=True)
     part = (log_rows / ND + log_cols / NG) / (2.0 * total_sel) - positive / total_sel
@@ -465,15 +482,18 @@
         total += dot(spread_t[0, :, rows_all:], far) + dot(spread_t[1, :, rows_all:], far)
         total += dot(hot, top[:, take], 0, 0) + dot(hot, mid[:, take], 0, 0)
         gn_ref[:, take] = total + dot(hot, low[:, take], 0, 0)
-
-    node_grads(0)
+        copy = pltpu.make_async_copy(gn_ref.at[:, take], gn_out.at[:, take], local_sem.at[2 + h])
+        copy.start()
+        return copy
+
+    out_copies = [node_grads(0)]
     arrived(copies)
     gfull[c, :, y, z] = gx[0] + gx[1] + gx[2] + gx[3]
     crossings = []
     weight_run = Plane(links, gfull.at[c]).gather(lambda view: crossings.append(links.core(view, view)))
     next(weight_run)
     next(weight_run)
-    node_grads(1)
+    out_copies.append(node_grads(1))
     text_dir = SCALE * tpart[x, c]
     gt_ref[...] = (
         text_dir - unit_texts * jnp.sum(unit_texts * text_dir, axis=1, keepdims=True)
@@ -481,48 +501,66 @@
     arrived(loss_copies)
     loss_ref[...] = jnp.sum(loss_grp[...], axis=0)[:1, :1]
     together(weight_run)
-    arrived(crossings)
-    deep = gfull.shape[4]
-    for e in range(ND):
-        for core in (0, 1):
-            for h in (0, 1):
-                start = (2 * e + core) * deep
-                gw_ref[start : start + deep, takes[h]] = gfull[core, h, e // 4, e % 4]
+    for i, core in enumerate((c, 1 - c)):
+        if i:
+            arrived(crossings)
+        copy = pltpu.make_async_copy(gfull.at[core], gw_out.at[core], local_sem.at[4 + i])
+        copy.start()
+        out_copies.append(copy)
     for copy in links.copies:
         copy.wait_send()
+    for copy in out_copies:
+        copy.wait()
+
+
+def finish_kernel(gn_in, gw_in, gt_in, gn_out, gw_out, gt_out, sem):
+    half = gw_in.shape[5]
+    rows = gn_in.shape[0] // 4
+    pairs = [(gn_in.at[pl.ds(i * rows, rows)], gn_out.at[pl.ds(i * rows, rows)]) for i in range(4)]
+    for core in (0, 1):
+        for h in (0, 1):
+            for y in range(4):
+                take = pl.ds(h * half, half)
+                pairs.append((gw_in.at[core, h, y], gw_out.at[y, :, core, :, take]))
+    pairs.append((gt_in, gt_out))
+    copies = [pltpu.make_async_copy(a, b, sem.at[i]) for i, (a, b) in enumerate(pairs)]
+    for copy in copies:
+        copy.start()
+    for copy in copies:
+        copy.wait()
 
 
 def shards(node_features, tiles, tile_list, weight, texts, selected, pairing):
-    device = lax.axis_index("grp") * ND + lax.axis_index("dev")
-    tile_dev, block = tiles.shape[0], tiles.shape[1]
+    block = tiles.shape[1]
     nodes_dev, feat = node_features.shape
     sel_dev = selected.shape[0]
     nb = nodes_dev // block
     half = feat // 2
     deep = feat // 32
-    my_list = lax.dynamic_slice_in_dim(tile_list, device * tile_dev, tile_dev, 0).reshape(-1)
     vmem = pl.BlockSpec(memory_space=pltpu.VMEM)
     smem = pl.BlockSpec(memory_space=pltpu.SMEM)
+    hbm = pl.BlockSpec(memory_space=pl.ANY)
     made = pl.pallas_call(
         prep_kernel,
         out_shape=(
             jax.ShapeDtypeStruct((3, NPEER + 1, sel_dev, block), BF16),
             jax.ShapeDtypeStruct((2, sel_dev, nb * block), BF16),
-            jax.ShapeDtypeStruct((nodes_dev, feat), BF16),
-            jax.ShapeDtypeStruct((sel_dev, feat), F32),
             jax.ShapeDtypeStruct((sel_dev, block), jnp.int32),
+            jax.ShapeDtypeStruct((sel_dev,), jnp.int32),
         ),
-        in_specs=[smem, smem, smem, vmem, vmem],
-        out_specs=(vmem,) * 5,
+        in_specs=[hbm, smem, smem, vmem],
+        out_specs=(vmem, vmem, vmem, smem),
         scratch_shapes=[
             pltpu.VMEM((nb, sel_dev, block), F32),
             pltpu.VMEM((nb, sel_dev, block), BF16),
             pltpu.VMEM((sel_dev, block), jnp.int32),
             pltpu.SMEM((NPEER + 1,), jnp.int32),
             pltpu.SMEM((NPEER + 1,), jnp.int32),
+            pltpu.SMEM((2, 256), jnp.int32),
+            pltpu.SemaphoreType.DMA,
         ],
         compiler_params=pltpu.CompilerParams(vmem_limit_bytes=60 * 2**20),
-    )(my_list, selected, pairing, tiles, node_features)
+    )(tile_list.T, selected, pairing, tiles)
 
     def f32(*shape):
         return pltpu.VMEM(shape, F32)
@@ -533,17 +571,21 @@
     plane = f32(2, 4, 4, sel_dev, half)
     landing = f32(2, 15, sel_dev, half)
     line = [f32(4, 2, sel_dev, feat), f32(4, sel_dev, feat), f32(3, sel_dev, feat)]
-    loss, grad_nodes, grad_weight, grad_texts = pl.pallas_call(
+    loss, *results = pl.pallas_call(
         main_kernel,
         out_shape=(
             jax.ShapeDtypeStruct((1, 1), F32),
             jax.ShapeDtypeStruct((nodes_dev, feat), F32),
-            jax.ShapeDtypeStruct((feat, feat), F32),
+            jax.ShapeDtypeStruct((2, 2, 4, 4, deep, half), F32),
             jax.ShapeDtypeStruct((sel_dev, feat), F32),
         ),
-        in_specs=[vmem] * 7,
-        out_specs=(vmem,) * 4,
+        in_specs=[vmem, vmem, vmem, smem, hbm, hbm, vmem],
+        out_specs=(vmem, hbm, hbm, vmem),
         scratch_shapes=[
+            f32(nodes_dev, feat),
+            f32(feat, feat),
+            bf16(nodes_dev, feat),
+            f32(nodes_dev, feat),
             bf16(3, ND, sel_dev, block),
             bf16(3, NG, sel_dev, block),
             bf16(2, NPEER, sel_dev, nb * block),
@@ -569,12 +611,25 @@
             f32(sel_dev, feat),
             pltpu.SemaphoreType.DMA((SEMS,)),
             pltpu.SemaphoreType.DMA((SEMS,)),
+            pltpu.SemaphoreType.DMA((6,)),
         ],
         compiler_params=pltpu.CompilerParams(
             collective_id=0, has_side_effects=True, vmem_limit_bytes=60 * 2**20
         ),
-    )(*made, weight, texts)
-    return loss.reshape(()), grad_nodes, grad_weight, grad_texts
+    )(*made, node_features, weight, texts)
+    grad_nodes, grad_weight, grad_texts = pl.pallas_call(
+        finish_kernel,
+        out_shape=(
+            jax.ShapeDtypeStruct((nodes_dev, feat), F32),
+            jax.ShapeDtypeStruct((4, 4, 2, deep, feat), F32),
+            jax.ShapeDtypeStruct((sel_dev, feat), F32),
+        ),
+        in_specs=[hbm] * 3,
+        out_specs=(hbm,) * 3,
+        scratch_shapes=[pltpu.SemaphoreType.DMA((21,))],
+        compiler_params=pltpu.CompilerParams(vmem_limit_bytes=60 * 2**20),
+    )(*results)
+    return loss.reshape(()), grad_nodes, grad_weight.reshape(feat, feat), grad_texts
 
 
 def solution(mesh):

time: 128 us -> 243 us (1.90)
  Pallas kernels: 119 us -> 241 us
  local copies, waits for them, and re-layouts: 6.33 us -> 0 us
    pallas_call x0 -> x1, Pallas kernels: none -> 123 us  [shards(): pl.pallas_call(finish_kernel, out_shape=(jax.ShapeDtypeStruct((nodes_dev,...]
    unnamed x9 -> x0, local copies, waits for them, and re-layouts: 5.51 us -> none
where the time goes in v4:
time: 243 us
  Pallas kernels  241 us (99%)
    pallas_call x1, Pallas kernels, shards(): pl.pallas_call(finish_kernel, out_shape=(jax.ShapeDtypeStruct((nodes_dev,...  123 us
    pallas_call x1, Pallas kernels, shards(): pl.pallas_call(main_kernel, out_shape=(jax.ShapeDtypeStruct((1, 1), F32),...  113 us

profile of v4, /device:TPU:1, one launch (start us, length us, event | category | flops | bytes accessed | tf_op | source)
XLA Modules:
  0.0 243.0 jit_solution(5194840073182361616)
XLA Ops:
  0.6 4.2 %shard_map.102 = (bf16[3,25,32,128]{3,2,1,0:T(8,128)(2,1)}, bf16[2,32,512]{2,1,0:T(8,128)(2,1)}, s32[32,128]{1,0:T(8,128)}, s32[32]{0:T(128)}) custom-call(s32[2,6656]{1,0:T(2,128)} %bitcast.3, s32[32]{0:T(128)} %sel_ref.1, s32[32]{0:T(128)} %pair_ref.1, bf16[52,128,128]{2,1,0:T(8,128)(2,1)} %tiles_ref.1), custom_call_target="tpu_custom_call" | custom-call | tf_op jit(solution)/shard_map/pallas_call | solution.py:543
  4.8 113.0 %shard_map.103 = (f32[1,1]{1,0:T(1,128)}, f32[512,768]{1,0:T(8,128)}, f32[2,2,4,4,24,384]{5,4,3,2,1,0:T(8,128)}, f32[32,768]{1,0:T(8,128)}) custom-call(bf16[3,25,32,128]{3,2,1,0:T(8,128)(2,1)} %get-tuple-element.15.rows_ref, bf16[2,32,512]{2,1,0:T(8,128)(2,1)} %get-tuple-element.16.local_ref, s32[32,128]{1,0:T(8,128)} %get-tuple-element.17.spot_ref, ...), custom_call_target="tpu_custom_call" | custom-call | tf_op jit(solution)/shard_map/pallas_call | solution.py:574
  117.8 123.4 %shard_map.104 = (f32[512,768]{1,0:T(8,128)}, f32[4,4,2,24,768]{4,3,2,1,0:T(8,128)}, f32[32,768]{1,0:T(8,128)}) custom-call(f32[512,768]{1,0:T(8,128)} %get-tuple-element.20.gn_in, f32[2,2,4,4,24,384]{5,4,3,2,1,0:T(8,128)} %get-tuple-element.21.gw_in, f32[32,768]{1,0:T(8,128)} %get-tuple-element.22.gt_in), custom_call_target="tpu_custom_call" | custom-call | tf_op jit(solution)/shard_map/pallas_call | solution.py:620

commit v5 on v4

--- a/solution.py
+++ b/solution.py
@@ -513,20 +513,28 @@
         copy.wait()
 
 
-def finish_kernel(gn_in, gw_in, gt_in, gn_out, gw_out, gt_out, sem):
+def finish_kernel(gn_in, gw_in, gt_in, gn_out, gw_out, gt_out, gn, gw, gt, in_sem, out_sem):
     half = gw_in.shape[5]
     rows = gn_in.shape[0] // 4
-    pairs = [(gn_in.at[pl.ds(i * rows, rows)], gn_out.at[pl.ds(i * rows, rows)]) for i in range(4)]
+    steps = []
+    for i in range(4):
+        some = pl.ds(i * rows, rows)
+        steps.append((gn_in.at[some], gn.at[some], gn_out.at[some]))
     for core in (0, 1):
         for h in (0, 1):
-            for y in range(4):
-                take = pl.ds(h * half, half)
-                pairs.append((gw_in.at[core, h, y], gw_out.at[y, :, core, :, take]))
-    pairs.append((gt_in, gt_out))
-    copies = [pltpu.make_async_copy(a, b, sem.at[i]) for i, (a, b) in enumerate(pairs)]
-    for copy in copies:
+            for y in (0, 2):
+                some = pl.ds(y, 2)
+                out = gw_out.at[some, :, core, :, pl.ds(h * half, half)]
+                steps.append((gw_in.at[core, h, some], gw.at[core, h, some], out))
+    steps.append((gt_in, gt, gt_out))
+    fetches = [pltpu.make_async_copy(a, b, in_sem.at[i]) for i, (a, b, _) in enumerate(steps)]
+    stores = [pltpu.make_async_copy(b, c, out_sem.at[i]) for i, (_, b, c) in enumerate(steps)]
+    for copy in fetches:
         copy.start()
-    for copy in copies:
+    for fetch, store in zip(fetches, stores):
+        fetch.wait()
+        store.start()
+    for copy in stores:
         copy.wait()
 
 
@@ -626,7 +634,13 @@
         ),
         in_specs=[hbm] * 3,
         out_specs=(hbm,) * 3,
-        scratch_shapes=[pltpu.SemaphoreType.DMA((21,))],
+        scratch_shapes=[
+            f32(nodes_dev, feat),
+            f32(2, 2, 4, 4, deep, half),
+            f32(sel_dev, feat),
+            pltpu.SemaphoreType.DMA((13,)),
+            pltpu.SemaphoreType.DMA((13,)),
+        ],
         compiler_params=pltpu.CompilerParams(vmem_limit_bytes=60 * 2**20),
     )(*results)
     return loss.reshape(()), grad_nodes, grad_weight.reshape(feat, feat), grad_texts

time: 243 us -> 123 us (0.51)
  Pallas kernels: 241 us -> 121 us
    pallas_call x1, Pallas kernels: 123 us -> 3.45 us  [shards(): pl.pallas_call(finish_kernel, out_shape=(jax.ShapeDtypeStruct((nodes_dev,...]
where the time goes in v5:
time: 123 us
  Pallas kernels  121 us (98%)
  between operations  2.41 us (2%)
    pallas_call x1, Pallas kernels, shards(): pl.pallas_call(main_kernel, out_shape=(jax.ShapeDtypeStruct((1, 1), F32),...  113 us
    pallas_call x1, Pallas kernels, shards(): pl.pallas_call(prep_kernel, out_shape=(jax.ShapeDtypeStruct((3, NPEER + 1...  4.18 us
    pallas_call x1, Pallas kernels, shards(): pl.pallas_call(finish_kernel, out_shape=(jax.ShapeDtypeStruct((nodes_dev,...  3.45 us

profile of v5, /device:TPU:1, one launch (start us, length us, event | category | flops | bytes accessed | tf_op | source)
XLA Modules:
  0.0 123.0 jit_solution(2781170533654173732)
XLA Ops:
  0.6 4.2 %shard_map.102 = (bf16[3,25,32,128]{3,2,1,0:T(8,128)(2,1)}, bf16[2,32,512]{2,1,0:T(8,128)(2,1)}, s32[32,128]{1,0:T(8,128)}, s32[32]{0:T(128)}) custom-call(s32[2,6656]{1,0:T(2,128)} %bitcast.3, s32[32]{0:T(128)} %sel_ref.1, s32[32]{0:T(128)} %pair_ref.1, bf16[52,128,128]{2,1,0:T(8,128)(2,1)} %tiles_ref.1), custom_call_target="tpu_custom_call" | custom-call | tf_op jit(solution)/shard_map/pallas_call | solution.py:551
  4.8 113.0 %shard_map.103 = (f32[1,1]{1,0:T(1,128)}, f32[512,768]{1,0:T(8,128)}, f32[2,2,4,4,24,384]{5,4,3,2,1,0:T(8,128)}, f32[32,768]{1,0:T(8,128)}) custom-call(bf16[3,25,32,128]{3,2,1,0:T(8,128)(2,1)} %get-tuple-element.15.rows_ref, bf16[2,32,512]{2,1,0:T(8,128)(2,1)} %get-tuple-element.16.local_ref, s32[32,128]{1,0:T(8,128)} %get-tuple-element.17.spot_ref, ...), custom_call_target="tpu_custom_call" | custom-call | tf_op jit(solution)/shard_map/pallas_call | solution.py:582
  117.8 3.5 %shard_map.104 = (f32[512,768]{1,0:T(8,128)}, f32[4,4,2,24,768]{4,3,2,1,0:T(8,128)}, f32[32,768]{1,0:T(8,128)}) custom-call(f32[512,768]{1,0:T(8,128)} %get-tuple-element.20.gn_in, f32[2,2,4,4,24,384]{5,4,3,2,1,0:T(8,128)} %get-tuple-element.21.gw_in, f32[32,768]{1,0:T(8,128)} %get-tuple-element.22.gt_in), custom_call_target="tpu_custom_call" | custom-call | tf_op jit(solution)/shard_map/pallas_call | solution.py:628

commit v6 on v5

--- a/solution.py
+++ b/solution.py
@@ -161,7 +161,7 @@
         into = (links.pos(self.inner[h]) + into) % 4
         return self.buf.at[0, out, into] if h == 0 else self.buf.at[1, into, out]
 
-    def gather(self, cross=None):
+    def gather(self, on=lambda h, out: None):
         shift, at, outer, inner = self.links.shift, self.at, self.outer, self.inner
         near, away = {}, {}
 
@@ -181,16 +181,14 @@
             for h in (0, 1):
                 near[h, i].wait_recv()
                 send_out(h, 4 - i)
-        if cross:
-            for h in (0, 1):
-                cross(at(h, 0, None))
-        yield
+        yield
+        for h in (0, 1):
+            on(h, 0)
         for i in (2, 1, 3):
             for h in (0, 1):
                 for o in (0, 2, 3, 1):
                     away[h, i, o].wait_recv()
-                if cross:
-                    cross(at(h, 4 - i, None))
+                on(h, 4 - i)
         yield
 
     def reduce(self, land):
@@ -280,7 +278,8 @@
     near_in, far_in, spread, spread_t, wh, wl,
     npart, nland, fpart, fpair, fsmall,
     units, cols, spart, sland, tpart, tpair, tsmall,
-    row_in, col_in, loss_dev, loss_grp, slices_out, slices, pre_all, pre_stack, g_far,
+    row_in, col_in, loss_dev, loss_grp, slices_out, slices, pre_all, g_far,
+    u_hi, u_lo, p_hi, p_lo, score_ref,
     gpart, gpair, gx, gfull, chosen,
     send_sem, recv_sem, local_sem,
 ):
@@ -311,9 +310,7 @@
     text_norm = jnp.sqrt(jnp.sum(texts * texts, axis=1, keepdims=True) + EPS)
     unit_texts = texts / text_norm
     cols[x, c] = unit_texts
-    near_in[:2, d] = jnp.zeros((2, sel_dev, block), BF16)
     near_in[2, d] = rows_ref[2, d]
-    far_in[:, g] = jnp.zeros((3, sel_dev, block), BF16)
     pl.semaphore_wait(barrier, ND + NG - 2)
 
     near_copies = links.all_dev(lambda e: rows_ref.at[:, e], near_in.at[:, d])
@@ -339,8 +336,9 @@
                     which == float(b), rows[q].astype(F32), 0.0
                 ).astype(BF16)
 
-    arrived(near_copies)
-    for p in range(ND):
+    for i, copy in enumerate(near_copies):
+        copy.wait_recv()
+        p = (d + ND - 1 - i) % ND
         expand(p, near_in[:, p])
     spread[0, d] = local_ref[0]
     spread[1, d] = local_ref[1]
@@ -351,9 +349,11 @@
         table = rounded[:, takes[h]]
         npart[h] = (dot(s0, table) + dot(s1, table)).reshape(4, 4, sel_dev, half)
         next(near_run)
-    arrived(far_copies)
-    for p in range(NG):
+    for i, copy in enumerate(far_copies):
+        copy.wait_recv()
+        p = (g + NG - 1 - i) % NG
         expand(ND + p, far_in[:, p])
+    spread[:, ND + g] = jnp.zeros((2, sel_dev, nb * block), BF16)
     flat = (cols_all, nb * block)
     s0, s1 = spread[0, ND:].reshape(flat), spread[1, ND:].reshape(flat)
     fpart[...] = (dot(s0, rounded[...]) + dot(s1, rounded[...])).reshape(4, 2, sel_dev, feat)
@@ -374,10 +374,19 @@
     unit_nodes = hidden / node_norm
     for h in (0, 1):
         units[h, y, z] = unit_nodes[:, takes[h]]
-    unit_run = Plane(links, units).gather()
-    next(unit_run)
     col_parts = split(cols[...].reshape(cols_all, feat))
     text_halves = [tuple(v[:, takes[h]] for v in col_parts) for h in (0, 1)]
+    some = 4 * sel_dev
+
+    def score(h, out):
+        parts = split(Plane(links, units).at(h, out, None)[...].reshape(some, half))
+        for v, into in zip(parts, (u_hi, u_lo)):
+            Plane(links, into).at(h, out, None)[...] = v.reshape(4, sel_dev, half)
+        part = dot3(parts, text_halves[h], 1, 1)
+        Plane(links, score_ref).at(h, out, None)[...] = part.reshape(4, sel_dev, cols_all)
+
+    unit_run = Plane(links, units).gather(score)
+    next(unit_run)
     next(unit_run)
     lane = lax.broadcasted_iota(jnp.int32, (8, cols_all), 1)
     ids = ((lane // sel_dev * ND + d) * sel_dev + lane % sel_dev)[:1]
@@ -390,9 +399,8 @@
     slices[d] = slices_out[d]
     together(unit_run)
 
-    unit_parts = [split(units[h].reshape(rows_all, half)) for h in (0, 1)]
-    scores = dot3(unit_parts[0], text_halves[0], 1, 1) + dot3(unit_parts[1], text_halves[1], 1, 1)
-    scores = SCALE * scores
+    unit_parts = [tuple(v[h].reshape(rows_all, half) for v in (u_hi, u_lo)) for h in (0, 1)]
+    scores = SCALE * (score_ref[0] + score_ref[1]).reshape(rows_all, cols_all)
     exps = jnp.exp(scores)
     row_in[d] = to_lanes(jnp.sum(exps, axis=1, keepdims=True))
     row_copies = links.all_dev(lambda e: row_in.at[d], row_in.at[d])
@@ -432,35 +440,40 @@
     pre_grad = node_back * (curve + before * jnp.exp(-0.5 * before * before) * INV_ROOT_TWO_PI)
     for h in (0, 1):
         pre_all[h, y, z] = pre_grad[:, takes[h]]
-    pre_run = Plane(links, pre_all).gather()
+    pieces = {0: 0.0, 1: 0.0}
+
+    def weigh(h, out):
+        hi, lo = split(Plane(links, pre_all).at(h, out, None)[...].reshape(some, half))
+        for v, into in ((hi, p_hi), (lo, p_lo)):
+            Plane(links, into).at(h, out, None)[...] = v.reshape(4, sel_dev, half)
+        across = ((y if h == 0 else z) + out) % 4
+        for k in range(4):
+            rows = slice(k * sel_dev, (k + 1) * sel_dev)
+            stack = jnp.concatenate([hi[rows], hi[rows], lo[rows], hi[rows]], axis=0)
+            p = across * 4 + k if h == 0 else k * 4 + across
+            pieces[h] += dot(slices[p], stack)
+
+    pre_run = Plane(links, pre_all).gather(weigh)
     next(pre_run)
     row_grads = dot3(split(pre_grad), (wh[...], wl[...]), 1, 1)
     g_far[x, c] = row_grads.astype(BF16)
     far_run = Line(links, g_far).gather()
     next(far_run)
+    arrived(slice_copies)
     next(pre_run)
     next(far_run)
     arrived(loss_copies)
     loss_grp[g] = jnp.sum(loss_dev[...], axis=0)
     loss_copies = links.all_grp(lambda e: loss_grp.at[g], loss_grp.at[g])
-    some = 128 // sel_dev
     for q in (0, 1):
-        for i in range(NPEER // some):
-            rows = spread[q, i * some : (i + 1) * some].reshape(128, nb * block)
-            spread_t[q, :, i * 128 : (i + 1) * 128] = rows.astype(F32).T.astype(BF16)
-    arrived(slice_copies)
+        for i in range(NPEER // 4):
+            rows = spread[q, 4 * i : 4 * i + 4].reshape(some, nb * block)
+            spread_t[q, :, i * some : (i + 1) * some] = rows.astype(F32).T.astype(BF16)
     together(pre_run, far_run)
 
-    pre_parts = []
+    pre_parts = [tuple(v[h].reshape(rows_all, half) for v in (p_hi, p_lo)) for h in (0, 1)]
     for h in (0, 1):
-        hi, lo = split(pre_all[h].reshape(rows_all, half))
-        pre_parts.append((hi, lo))
-        for i, v in enumerate((hi, hi, lo, hi)):
-            pre_stack[h, :, i] = v.reshape(ND, sel_dev, half)
-        piece = 0.0
-        for p in range(ND):
-            piece += dot(slices[p], pre_stack[h, p].reshape(4 * sel_dev, half))
-        gpart[:, h] = piece.reshape(2, piece.shape[0] // 2, half)
+        gpart[:, h] = pieces[h].reshape(2, pieces[h].shape[0] // 2, half)
     core_copy = links.core(gpart.at[1 - c], gpair)
     group_grads = dot3(pre_parts[0], (wh[:, takes[0]], wl[:, takes[0]]), 1, 1)
     group_grads += dot3(pre_parts[1], (wh[:, takes[1]], wl[:, takes[1]]), 1, 1)
@@ -490,7 +503,13 @@
     arrived(copies)
     gfull[c, :, y, z] = gx[0] + gx[1] + gx[2] + gx[3]
     crossings = []
-    weight_run = Plane(links, gfull.at[c]).gather(lambda view: crossings.append(links.core(view, view)))
+    weight_plane = Plane(links, gfull.at[c])
+
+    def cross(h, out):
+        view = weight_plane.at(h, out, None)
+        crossings.append(links.core(view, view))
+
+    weight_run = weight_plane.gather(cross)
     next(weight_run)
     next(weight_run)
     out_copies.append(node_grads(1))
@@ -513,7 +532,11 @@
         copy.wait()
 
 
-def finish_kernel(gn_in, gw_in, gt_in, gn_out, gw_out, gt_out, gn, gw, gt, in_sem, out_sem):
+def finish_kernel(
+    loss_in, gn_in, gw_in, gt_in,
+    loss_out, gn_out, gw_out, gt_out,
+    gn, gw, gt, in_sem, out_sem,
+):
     half = gw_in.shape[5]
     rows = gn_in.shape[0] // 4
     steps = []
@@ -531,6 +554,7 @@
     stores = [pltpu.make_async_copy(b, c, out_sem.at[i]) for i, (_, b, c) in enumerate(steps)]
     for copy in fetches:
         copy.start()
+    loss_out[...] = loss_in[...]
     for fetch, store in zip(fetches, stores):
         fetch.wait()
         store.start()
@@ -579,7 +603,7 @@
     plane = f32(2, 4, 4, sel_dev, half)
     landing = f32(2, 15, sel_dev, half)
     line = [f32(4, 2, sel_dev, feat), f32(4, sel_dev, feat), f32(3, sel_dev, feat)]
-    loss, *results = pl.pallas_call(
+    results = pl.pallas_call(
         main_kernel,
         out_shape=(
             jax.ShapeDtypeStruct((1, 1), F32),
@@ -610,8 +634,9 @@
             bf16(ND, 2 * deep, 4 * sel_dev),
             bf16(ND, 2 * deep, 4 * sel_dev),
             plane,
-            bf16(2, ND, 4, sel_dev, half),
             bf16(4, 2, sel_dev, feat),
+            *[bf16(2, 4, 4, sel_dev, half)] * 4,
+            f32(2, 4, 4, sel_dev, NG * sel_dev),
             f32(2, 2, deep, half),
             f32(2, deep, half),
             f32(4, 2, deep, half),
@@ -625,15 +650,16 @@
             collective_id=0, has_side_effects=True, vmem_limit_bytes=60 * 2**20
         ),
     )(*made, node_features, weight, texts)
-    grad_nodes, grad_weight, grad_texts = pl.pallas_call(
+    loss, grad_nodes, grad_weight, grad_texts = pl.pallas_call(
         finish_kernel,
         out_shape=(
+            jax.ShapeDtypeStruct((1, 1), F32),
             jax.ShapeDtypeStruct((nodes_dev, feat), F32),
             jax.ShapeDtypeStruct((4, 4, 2, deep, feat), F32),
             jax.ShapeDtypeStruct((sel_dev, feat), F32),
         ),
-        in_specs=[hbm] * 3,
-        out_specs=(hbm,) * 3,
+        in_specs=[vmem, hbm, hbm, hbm],
+        out_specs=(vmem, hbm, hbm, hbm),
         scratch_shapes=[
             f32(nodes_dev, feat),
             f32(2, 2, 4, 4, deep, half),

time: 123 us -> 122 us (level)
  between operations: 2.41 us -> 0.81 us
where the time goes in v6:
time: 122 us
  Pallas kernels  121 us (99%)
    pallas_call x1, Pallas kernels, shards(): pl.pallas_call(main_kernel, out_shape=(jax.ShapeDtypeStruct((1, 1), F32),...  113 us
    pallas_call x1, Pallas kernels, shards(): pl.pallas_call(finish_kernel, out_shape=(jax.ShapeDtypeStruct((1, 1), F32...  4.59 us
    pallas_call x1, Pallas kernels, shards(): pl.pallas_call(prep_kernel, out_shape=(jax.ShapeDtypeStruct((3, NPEER + 1...  4.18 us

profile of v6, /device:TPU:1, one launch (start us, length us, event | category | flops | bytes accessed | tf_op | source)
XLA Modules:
  0.0 122.2 jit_solution(16420305119149672020)
XLA Ops:
  0.6 4.2 %shard_map.102 = (bf16[3,25,32,128]{3,2,1,0:T(8,128)(2,1)}, bf16[2,32,512]{2,1,0:T(8,128)(2,1)}, s32[32,128]{1,0:T(8,128)}, s32[32]{0:T(128)}) custom-call(s32[2,6656]{1,0:T(2,128)} %bitcast.3, s32[32]{0:T(128)} %sel_ref.1, s32[32]{0:T(128)} %pair_ref.1, bf16[52,128,128]{2,1,0:T(8,128)(2,1)} %tiles_ref.1), custom_call_target="tpu_custom_call" | custom-call | tf_op jit(solution)/shard_map/pallas_call | solution.py:575
  4.8 112.6 %shard_map.103 = (f32[1,1]{1,0:T(1,128)}, f32[512,768]{1,0:T(8,128)}, f32[2,2,4,4,24,384]{5,4,3,2,1,0:T(8,128)}, f32[32,768]{1,0:T(8,128)}) custom-call(bf16[3,25,32,128]{3,2,1,0:T(8,128)(2,1)} %get-tuple-element.16.rows_ref, bf16[2,32,512]{2,1,0:T(8,128)(2,1)} %get-tuple-element.17.local_ref, s32[32,128]{1,0:T(8,128)} %get-tuple-element.18.spot_ref, ...), custom_call_target="tpu_custom_call" | custom-call | tf_op jit(solution)/shard_map/pallas_call | solution.py:606
  117.4 4.6 %shard_map.104 = (f32[1,1]{1,0:T(1,128)}, f32[512,768]{1,0:T(8,128)}, f32[4,4,2,24,768]{4,3,2,1,0:T(8,128)}, f32[32,768]{1,0:T(8,128)}) custom-call(f32[1,1]{1,0:T(1,128)} %get-tuple-element.20.loss_in, f32[512,768]{1,0:T(8,128)} %get-tuple-element.21.gn_in, f32[2,2,4,4,24,384]{5,4,3,2,1,0:T(8,128)} %get-tuple-element.22.gw_in, ...), custom_call_target="tpu_custom_call" | custom-call | tf_op jit(solution)/shard_map/pallas_call | solution.py:653

commit v7 on v6

--- a/solution.py
+++ b/solution.py
@@ -34,18 +34,26 @@
 
 
 def prep_kernel(
-    list_ref, sel_ref, pair_ref, tiles_ref,
+    list_ref, sel_ref, pair_ref, tiles_hbm,
     rows_ref, local_ref, spot_ref, own_ref,
-    acc, onehot, column, count, meta, window, sem,
+    acc, onehot, column, count, meta, window, tiles_ref, sem, tiles_sem,
 ):
     g, d = lax.axis_index("grp"), lax.axis_index("dev")
     device = g * ND + d
-    n_tiles, block = tiles_ref.shape[0], tiles_ref.shape[1]
+    n_tiles, block = tiles_hbm.shape[0], tiles_hbm.shape[1]
     wide = window.shape[1]
     first = jnp.minimum(device * n_tiles // 128 * 128, list_ref.shape[1] - wide)
     first = pl.multiple_of(first, 128)
     fetch = pltpu.make_async_copy(list_ref.at[:, pl.ds(first, wide)], window, sem)
     fetch.start()
+    chunk = n_tiles // 4
+    chunks = []
+    for i in range(4):
+        some = pl.ds(i * chunk, chunk)
+        chunks.append(
+            pltpu.make_async_copy(tiles_hbm.at[some], tiles_ref.at[some], tiles_sem.at[i])
+        )
+        chunks[i].start()
     sel_dev = sel_ref.shape[0]
     nb = local_ref.shape[2] // block
     nodes_dev = nb * block
@@ -66,6 +74,8 @@
     fetch.wait()
     skip = device * n_tiles - first
     for t in range(n_tiles):
+        if t % chunk == 0:
+            chunks[t // chunk].wait()
         row_block = window[0, skip + t] - device * nb
         col = window[1, skip + t]
         owner = col // nb
@@ -78,14 +88,18 @@
         count[peer] = rank + 1
         meta[peer] = meta[peer] + col_block * jnp.where(rank == 0, 1, nb)
         picked = dot(onehot[row_block], tiles_ref[t])
-        rows_ref[rank, peer] = picked.astype(BF16)
+        start = pl.multiple_of(rank * sel_dev, sel_dev)
+        rows_ref[peer, pl.ds(start, sel_dev)] = picked.astype(BF16)
         acc[col_block] += picked * local.astype(F32)
     pair = column[...]
     high = pair // 64
-    tag = jnp.where(lane == 1, high, pair - high * 64)
+    low = pair - high * 64
+    lane = lane[:16]
+    tag = jnp.where(lane == 1, high[:16], low[:16])
+    tag = jnp.where(lane == 3, high[16:], jnp.where(lane == 4, low[16:], tag))
+    tail = pl.ds(2 * sel_dev, 16)
     for p in range(NPEER):
-        rows_ref[2, p] = jnp.where(lane == 0, meta[p], tag).astype(F32).astype(BF16)
-    rows_ref[2, d] = jnp.where(lane == 0, 0, tag).astype(F32).astype(BF16)
+        rows_ref[p, tail] = jnp.where(lane == 0, meta[p], tag).astype(F32).astype(BF16)
     for b in range(nb):
         hi, lo = split(acc[b])
         local_ref[0, :, b * block : (b + 1) * block] = hi
@@ -288,7 +302,7 @@
     sel_dev, feat = texts_ref.shape
     half = feat // 2
     nodes_dev = nodes_ref.shape[0]
-    block = near_in.shape[3]
+    block = near_in.shape[2]
     nb = nodes_dev // block
     total_sel = sel_dev * NG * ND
     rows_all = ND * sel_dev
@@ -310,11 +324,11 @@
     text_norm = jnp.sqrt(jnp.sum(texts * texts, axis=1, keepdims=True) + EPS)
     unit_texts = texts / text_norm
     cols[x, c] = unit_texts
-    near_in[2, d] = rows_ref[2, d]
+    near_in[d] = rows_ref[d]
     pl.semaphore_wait(barrier, ND + NG - 2)
 
-    near_copies = links.all_dev(lambda e: rows_ref.at[:, e], near_in.at[:, d])
-    far_copies = links.all_grp(lambda e: rows_ref.at[:, ND + e], far_in.at[:, g])
+    near_copies = links.all_dev(lambda e: rows_ref.at[e], near_in.at[d])
+    far_copies = links.all_grp(lambda e: rows_ref.at[ND + e], far_in.at[g])
     text_run = Line(links, cols).gather()
     next(text_run)
     nodes_copy.wait()
@@ -327,19 +341,19 @@
     wl[...] = lo
 
     def expand(into, rows):
-        tag = rows[2].astype(F32)[:, :1]
+        tag = rows[2 * sel_dev :].astype(F32)[:1, :1]
         second = jnp.floor(tag * (1.0 / nb) + 0.01)
         first = tag - second * nb
         for q, which in ((0, first), (1, second)):
             for b in range(nb):
                 spread[q, into, :, b * block : (b + 1) * block] = jnp.where(
-                    which == float(b), rows[q].astype(F32), 0.0
+                    which == float(b), rows[q * sel_dev : (q + 1) * sel_dev].astype(F32), 0.0
                 ).astype(BF16)
 
     for i, copy in enumerate(near_copies):
         copy.wait_recv()
         p = (d + ND - 1 - i) % ND
-        expand(p, near_in[:, p])
+        expand(p, near_in[p])
     spread[0, d] = local_ref[0]
     spread[1, d] = local_ref[1]
     flat = (rows_all, nb * block)
@@ -352,7 +366,7 @@
     for i, copy in enumerate(far_copies):
         copy.wait_recv()
         p = (g + NG - 1 - i) % NG
-        expand(ND + p, far_in[:, p])
+        expand(ND + p, far_in[p])
     spread[:, ND + g] = jnp.zeros((2, sel_dev, nb * block), BF16)
     flat = (cols_all, nb * block)
     s0, s1 = spread[0, ND:].reshape(flat), spread[1, ND:].reshape(flat)
@@ -390,8 +404,10 @@
     next(unit_run)
     lane = lax.broadcasted_iota(jnp.int32, (8, cols_all), 1)
     ids = ((lane // sel_dev * ND + d) * sel_dev + lane % sel_dev)[:1]
-    tags = near_in[2].reshape(rows_all, block).astype(F32)
-    target = (tags[:, 1:2] * 64.0 + tags[:, 2:3] == ids.astype(F32)).astype(F32)
+    tags = near_in[:, 2 * sel_dev :].astype(F32)
+    parts = [tags[:, :, k : k + 1] * 64.0 + tags[:, :, k + 1 : k + 2] for k in (1, 3)]
+    pair = jnp.concatenate(parts, axis=1).reshape(rows_all, 1)
+    target = (pair == ids.astype(F32)).astype(F32)
     wide = jnp.concatenate(
         [v.astype(F32) for v in (*picked_parts, picked_parts[0])] + [jnp.zeros_like(picked)], axis=0
     )
@@ -575,12 +591,12 @@
     made = pl.pallas_call(
         prep_kernel,
         out_shape=(
-            jax.ShapeDtypeStruct((3, NPEER + 1, sel_dev, block), BF16),
+            jax.ShapeDtypeStruct((NPEER + 1, 2 * sel_dev + 16, block), BF16),
             jax.ShapeDtypeStruct((2, sel_dev, nb * block), BF16),
             jax.ShapeDtypeStruct((sel_dev, block), jnp.int32),
             jax.ShapeDtypeStruct((sel_dev,), jnp.int32),
         ),
-        in_specs=[hbm, smem, smem, vmem],
+        in_specs=[hbm, smem, smem, hbm],
         out_specs=(vmem, vmem, vmem, smem),
         scratch_shapes=[
             pltpu.VMEM((nb, sel_dev, block), F32),
@@ -589,7 +605,9 @@
             pltpu.SMEM((NPEER + 1,), jnp.int32),
             pltpu.SMEM((NPEER + 1,), jnp.int32),
             pltpu.SMEM((2, 256), jnp.int32),
+            pltpu.VMEM(tiles.shape, BF16),
             pltpu.SemaphoreType.DMA,
+            pltpu.SemaphoreType.DMA((4,)),
         ],
         compiler_params=pltpu.CompilerParams(vmem_limit_bytes=60 * 2**20),
     )(tile_list.T, selected, pairing, tiles)
@@ -618,8 +636,8 @@
             f32(feat, feat),
             bf16(nodes_dev, feat),
             f32(nodes_dev, feat),
-            bf16(3, ND, sel_dev, block),
-            bf16(3, NG, sel_dev, block),
+            bf16(ND, 2 * sel_dev + 16, block),
+            bf16(NG, 2 * sel_dev + 16, block),
             bf16(2, NPEER, sel_dev, nb * block),
             bf16(2, nb * block, NPEER * sel_dev),
             bf16(feat, feat),

time: 122 us -> 121 us (level)
    pallas_call x1, Pallas kernels: 113 us -> 111 us  [shards(): pl.pallas_call(main_kernel, out_shape=(jax.ShapeDtypeStruct((1, 1), F32),...]
where the time goes in v7:
time: 121 us; the launch traced here: 120 us
  Pallas kernels  120 us (99%)
    pallas_call x1, Pallas kernels, shards(): pl.pallas_call(main_kernel, out_shape=(jax.ShapeDtypeStruct((1, 1), F32),...  111 us
    pallas_call x1, Pallas kernels, shards(): pl.pallas_call(finish_kernel, out_shape=(jax.ShapeDtypeStruct((1, 1), F32...  4.59 us
    pallas_call x1, Pallas kernels, shards(): pl.pallas_call(prep_kernel, out_shape=(jax.ShapeDtypeStruct((NPEER + 1, 2...  3.71 us

profile of v7, /device:TPU:1, one launch (start us, length us, event | category | flops | bytes accessed | tf_op | source)
XLA Modules:
  0.0 120.4 jit_solution(6454214733414072936)
XLA Ops:
  0.6 3.7 %shard_map.102 = (bf16[25,80,128]{2,1,0:T(8,128)(2,1)}, bf16[2,32,512]{2,1,0:T(8,128)(2,1)}, s32[32,128]{1,0:T(8,128)}, s32[32]{0:T(128)}) custom-call(s32[2,6656]{1,0:T(2,128)} %bitcast.3, s32[32]{0:T(128)} %sel_ref.1, s32[32]{0:T(128)} %pair_ref.1, bf16[52,128,128]{2,1,0:T(8,128)(2,1)} %tiles_hbm.1), custom_call_target="tpu_custom_call" | custom-call | tf_op jit(solution)/shard_map/pallas_call | solution.py:591
  4.4 111.3 %shard_map.103 = (f32[1,1]{1,0:T(1,128)}, f32[512,768]{1,0:T(8,128)}, f32[2,2,4,4,24,384]{5,4,3,2,1,0:T(8,128)}, f32[32,768]{1,0:T(8,128)}) custom-call(bf16[25,80,128]{2,1,0:T(8,128)(2,1)} %get-tuple-element.16.rows_ref, bf16[2,32,512]{2,1,0:T(8,128)(2,1)} %get-tuple-element.17.local_ref, s32[32,128]{1,0:T(8,128)} %get-tuple-element.18.spot_ref, ...), custom_call_target="tpu_custom_call" | custom-call | tf_op jit(solution)/shard_map/pallas_call | solution.py:624
  115.6 4.6 %shard_map.104 = (f32[1,1]{1,0:T(1,128)}, f32[512,768]{1,0:T(8,128)}, f32[4,4,2,24,768]{4,3,2,1,0:T(8,128)}, f32[32,768]{1,0:T(8,128)}) custom-call(f32[1,1]{1,0:T(1,128)} %get-tuple-element.20.loss_in, f32[512,768]{1,0:T(8,128)} %get-tuple-element.21.gn_in, f32[2,2,4,4,24,384]{5,4,3,2,1,0:T(8,128)} %get-tuple-element.22.gw_in, ...), custom_call_target="tpu_custom_call" | custom-call | tf_op jit(solution)/shard_map/pallas_call | solution.py:671

commit v8 on v7

--- a/solution.py
+++ b/solution.py
@@ -515,26 +515,25 @@
         copy.start()
         return copy
 
-    out_copies = [node_grads(0)]
-    arrived(copies)
-    gfull[c, :, y, z] = gx[0] + gx[1] + gx[2] + gx[3]
-    crossings = []
-    weight_plane = Plane(links, gfull.at[c])
-
-    def cross(h, out):
-        view = weight_plane.at(h, out, None)
-        crossings.append(links.core(view, view))
-
-    weight_run = weight_plane.gather(cross)
-    next(weight_run)
-    next(weight_run)
-    out_copies.append(node_grads(1))
+    out_copies = [node_grads(0), node_grads(1)]
     text_dir = SCALE * tpart[x, c]
     gt_ref[...] = (
         text_dir - unit_texts * jnp.sum(unit_texts * text_dir, axis=1, keepdims=True)
     ) / text_norm
     arrived(loss_copies)
     loss_ref[...] = jnp.sum(loss_grp[...], axis=0)[:1, :1]
+    arrived(copies)
+    gfull[c, :, y, z] = gx[0] + gx[1] + gx[2] + gx[3]
+    crossings = []
+    weight_plane = Plane(links, gfull.at[c])
+
+    def cross(h, out):
+        view = weight_plane.at(h, out, None)
+        crossings.append(links.core(view, view))
+
+    weight_run = weight_plane.gather(cross)
+    next(weight_run)
+    next(weight_run)
     together(weight_run)
     for i, core in enumerate((c, 1 - c)):
         if i:

time: 121 us -> 120 us (level)
  no operation moved by 1% of the time
where the time goes in v8:
time: 120 us
  Pallas kernels  119 us (99%)
    pallas_call x1, Pallas kernels, shards(): pl.pallas_call(main_kernel, out_shape=(jax.ShapeDtypeStruct((1, 1), F32),...  111 us
    pallas_call x1, Pallas kernels, shards(): pl.pallas_call(finish_kernel, out_shape=(jax.ShapeDtypeStruct((1, 1), F32...  4.59 us
    pallas_call x1, Pallas kernels, shards(): pl.pallas_call(prep_kernel, out_shape=(jax.ShapeDtypeStruct((NPEER + 1, 2...  3.71 us

profile of v8, /device:TPU:1, one launch (start us, length us, event | category | flops | bytes accessed | tf_op | source)
XLA Modules:
  0.0 120.2 jit_solution(10952479667885196265)
XLA Ops:
  0.6 3.7 %shard_map.102 = (bf16[25,80,128]{2,1,0:T(8,128)(2,1)}, bf16[2,32,512]{2,1,0:T(8,128)(2,1)}, s32[32,128]{1,0:T(8,128)}, s32[32]{0:T(128)}) custom-call(s32[2,6656]{1,0:T(2,128)} %bitcast.3, s32[32]{0:T(128)} %sel_ref.1, s32[32]{0:T(128)} %pair_ref.1, bf16[52,128,128]{2,1,0:T(8,128)(2,1)} %tiles_hbm.1), custom_call_target="tpu_custom_call" | custom-call | tf_op jit(solution)/shard_map/pallas_call | solution.py:590
  4.4 111.1 %shard_map.103 = (f32[1,1]{1,0:T(1,128)}, f32[512,768]{1,0:T(8,128)}, f32[2,2,4,4,24,384]{5,4,3,2,1,0:T(8,128)}, f32[32,768]{1,0:T(8,128)}) custom-call(bf16[25,80,128]{2,1,0:T(8,128)(2,1)} %get-tuple-element.16.rows_ref, bf16[2,32,512]{2,1,0:T(8,128)(2,1)} %get-tuple-element.17.local_ref, s32[32,128]{1,0:T(8,128)} %get-tuple-element.18.spot_ref, ...), custom_call_target="tpu_custom_call" | custom-call | tf_op jit(solution)/shard_map/pallas_call | solution.py:623
  115.5 4.6 %shard_map.104 = (f32[1,1]{1,0:T(1,128)}, f32[512,768]{1,0:T(8,128)}, f32[4,4,2,24,768]{4,3,2,1,0:T(8,128)}, f32[32,768]{1,0:T(8,128)}) custom-call(f32[1,1]{1,0:T(1,128)} %get-tuple-element.20.loss_in, f32[512,768]{1,0:T(8,128)} %get-tuple-element.21.gn_in, f32[2,2,4,4,24,384]{5,4,3,2,1,0:T(8,128)} %get-tuple-element.22.gw_in, ...), custom_call_target="tpu_custom_call" | custom-call | tf_op jit(solution)/shard_map/pallas_call | solution.py:670
